TPU v7x, 32 devices: a whole 2x2x4 slice. The times are simulated.
32 devices in a mesh: seq: 4 (over y, x), fsdp: 8 (over z, core).
Axes of the slice: x: 2, y: 2, z: 4, core: 2. Of those that a mesh axis runs over, the one named last changes fastest.
Arguments:
- tokens: bfloat16 [8, 512, 1024], P('fsdp', 'seq'), may hold values from -6 to 6
- attn_gain: float32 [1024], replicated, may hold values from 0.25 to 1.75
- w_query: bfloat16 [1024, 1024], P(('seq', 'fsdp')), may hold values from -0.1875 to 0.1875
- w_key: bfloat16 [1024, 1024], P(('seq', 'fsdp')), may hold values from -0.1875 to 0.1875
- value_weight: bfloat16 [1024, 2048], P(('seq', 'fsdp')), may hold values from -0.1875 to 0.1875
- w_gate: bfloat16 [1024, 2048], P(('seq', 'fsdp')), may hold values from -0.1875 to 0.1875
- w_beta: bfloat16 [1024, 8], P(('seq', 'fsdp')), may hold values from -0.1875 to 0.1875
- w_decay: bfloat16 [1024, 8], P(('seq', 'fsdp')), may hold values from -0.1875 to 0.1875
- conv_query: float32 [4, 1024], replicated, may hold values from -2 to 2
- conv_key: float32 [4, 1024], replicated, may hold values from -2 to 2
- conv_value: float32 [4, 2048], replicated, may hold values from -2 to 2
- decay_rate: float32 [8], replicated, may hold values from 0 to 1, as said below
- decay_bias: float32 [8], replicated, may hold values from -1 to 1
- out_gain: float32 [256], replicated, may hold values from 0.25 to 1.75
- w_out: bfloat16 [2048, 1024], P(('seq', 'fsdp')), may hold values from -0.125 to 0.125
- mlp_gain: float32 [1024], replicated, may hold values from 0.25 to 1.75
- w_mlp_gate: bfloat16 [1024, 2816], P(('seq', 'fsdp')), may hold values from -0.1875 to 0.1875
- w_up: bfloat16 [1024, 2816], P(('seq', 'fsdp')), may hold values from -0.1875 to 0.1875
- w_down: bfloat16 [2816, 1024], P(('seq', 'fsdp')), may hold values from -0.109375 to 0.109375
- cotangent: bfloat16 [8, 512, 1024], P('fsdp', 'seq'), may hold values from -6 to 6
Outputs:
- output: bfloat16 [8, 512, 1024], P('fsdp', 'seq')
- grad_tokens: float32 [8, 512, 1024], P('fsdp', 'seq')
- grad_attn_gain: float32 [1024], replicated
- grad_w_query: float32 [1024, 1024], P(('seq', 'fsdp'))
- grad_w_key: float32 [1024, 1024], P(('seq', 'fsdp'))
- grad_w_value: float32 [1024, 2048], P(('seq', 'fsdp'))
- grad_w_gate: float32 [1024, 2048], P(('seq', 'fsdp'))
- grad_w_beta: float32 [1024, 8], P(('seq', 'fsdp'))
- grad_w_decay: float32 [1024, 8], P(('seq', 'fsdp'))
- grad_conv_query: float32 [4, 1024], replicated
- grad_conv_key: float32 [4, 1024], replicated
- grad_conv_value: float32 [4, 2048], replicated
- grad_decay_rate: float32 [8], replicated
- grad_decay_bias: float32 [8], replicated
- grad_out_gain: float32 [256], replicated
- grad_w_out: float32 [2048, 1024], P(('seq', 'fsdp'))
- grad_mlp_gain: float32 [1024], replicated
- grad_w_mlp_gate: float32 [1024, 2816], P(('seq', 'fsdp'))
- grad_w_up: float32 [1024, 2816], P(('seq', 'fsdp'))
- grad_w_down: float32 [2816, 1024], P(('seq', 'fsdp'))
Inputs may be any that keep to these rules, and one draw needn't show every extreme that they name: `decay_rate`: positive decay rates.
All inputs are finite; a program needn't handle non-finite values.
Results may differ from a plain program's by a relative error of at most 0.015.
The roundings to bfloat16 on the way count: a program that leaves them out, or rounds other values in their place, can miss the bound.
Values may be sent and summed in bfloat16 or wider, within the bound.
A program may use at most 256 MiB of HBM per device.

v0:
```python
import jax
import jax.numpy as jnp
from jax import lax
from jax.sharding import PartitionSpec as P

GROUP = 64


epsilon = 1e-06
highest_precision = lax.Precision.HIGHEST


def product(left, right):
    return jnp.dot(left, right, precision=highest_precision)


def bf_dot(left, right):
    return jnp.dot(left, right, preferred_element_type=jnp.float32)


def rms_scale(signal, gain):
    return signal * lax.rsqrt(jnp.mean(signal * signal, axis=-1, keepdims=True) + epsilon) * gain


def unit_rows(signal):
    return signal * lax.rsqrt(jnp.sum(signal * signal, axis=-1, keepdims=True) + epsilon)


def causal_conv(signal, kernel):
    length = signal.shape[-2]
    taps = kernel.shape[0]
    padding = [(0, 0)] * (signal.ndim - 2) + [(taps - 1, 0), (0, 0)]
    padded = jnp.pad(signal, padding)
    summed = jnp.zeros_like(signal)
    for offset in range(taps):
        summed = summed + kernel[offset] * lax.slice_in_dim(
            padded, offset, offset + length, axis=signal.ndim - 2
        )
    return summed


def block_step(memory, inputs):
    query_rows, key_rows, value_rows, strength, log_decay = inputs
    block_len = query_rows.shape[0]
    key_width = key_rows.shape[1]
    cumulative = jnp.cumsum(log_decay)
    causal = jnp.tril(jnp.ones((block_len, block_len), dtype=bool))
    strict = jnp.tril(jnp.ones((block_len, block_len), dtype=bool), -1)
    decay_pair = jnp.where(
        causal, jnp.exp(jnp.where(causal, cumulative[:, None] - cumulative[None, :], 0.0)), 0.0
    )
    key_gram = product(key_rows, key_rows.T)
    system = jnp.eye(block_len, dtype=jnp.float32) + jnp.where(
        strict, strength[:, None] * key_gram * decay_pair, 0.0
    )
    from_start = jnp.exp(cumulative)[:, None]
    right_side = jnp.concatenate(
        [strength[:, None] * from_start * key_rows, strength[:, None] * value_rows], axis=1
    )
    solved = jax.scipy.linalg.solve_triangular(system, right_side, lower=True, unit_diagonal=True)
    corrected = solved[:, key_width:] - product(solved[:, :key_width], memory)
    scores = jnp.where(causal, product(query_rows, key_rows.T) * decay_pair, 0.0)
    outputs = from_start * product(query_rows, memory) + product(scores, corrected)
    to_end = jnp.exp(cumulative[-1] - cumulative)[:, None]
    memory = jnp.exp(cumulative[-1]) * memory + product((key_rows * to_end).T, corrected)
    return (memory, outputs)


def delta_blocks(query_rows, key_rows, value_rows, strength, log_decay):
    length = query_rows.shape[0]
    blocks = length // GROUP
    shaped = tuple(
        (
            t.reshape((blocks, GROUP) + t.shape[1:])
            for t in (query_rows, key_rows, value_rows, strength, log_decay)
        )
    )
    memory = jnp.zeros((key_rows.shape[1], value_rows.shape[1]), jnp.float32)
    _, outputs = lax.scan(jax.checkpoint(block_step), memory, shaped)
    return outputs.reshape(length, value_rows.shape[1])


def head_piece(query_in, key_in, value_in, gate_logits, conv_q, conv_k, conv_v, rate, bias):
    batches, length, local, head_k = query_in.shape
    head_v = value_in.shape[3]
    queries = jax.nn.silu(
        causal_conv(query_in.reshape(batches, length, local * head_k), conv_q)
    ).reshape(query_in.shape)
    queries = unit_rows(queries) * head_k ** (-0.5)
    keys_all = unit_rows(
        jax.nn.silu(causal_conv(key_in.reshape(batches, length, local * head_k), conv_k)).reshape(
            key_in.shape
        )
    )
    values_all = jax.nn.silu(
        causal_conv(value_in.reshape(batches, length, local * head_v), conv_v)
    ).reshape(value_in.shape)
    strength = jax.nn.sigmoid(gate_logits[..., 0])
    log_decay = -rate * jax.nn.softplus(gate_logits[..., 1] + bias)

    def by_head(values):
        return jnp.moveaxis(values, 2, 1).reshape((batches * local, length) + values.shape[3:])

    mixed = jax.vmap(delta_blocks)(
        by_head(queries),
        by_head(keys_all),
        by_head(values_all),
        by_head(strength),
        by_head(log_decay),
    )
    return jnp.moveaxis(mixed.reshape(batches, local, length, head_v), 1, 2)


def out_piece(values, gate_values, gain):
    return rms_scale(values, gain) * jax.nn.silu(gate_values)


def swish_piece(gate_values, up_values):
    return jax.nn.silu(gate_values) * up_values


def widen(part, whole_shape, offset):
    return lax.dynamic_update_slice_in_dim(
        jnp.zeros(whole_shape, jnp.float32), part, offset, part.ndim - 1
    )


def column_term(left, right):
    return bf_dot(left.T, right)


def on_device(
    tokens,
    attn_gain,
    w_query,
    w_key,
    value_weight,
    w_gate,
    w_beta,
    w_decay,
    conv_query,
    conv_key,
    conv_value,
    decay_rate,
    decay_bias,
    out_gain,
    w_out,
    mlp_gain,
    w_mlp_gate,
    w_up,
    w_down,
    cotangent,
):
    shards = (
        w_query,
        w_key,
        value_weight,
        w_gate,
        w_beta,
        w_decay,
        w_out,
        w_mlp_gate,
        w_up,
        w_down,
    )
    gathered = (
        lax.all_gather(shards[0], ("seq", "fsdp"), axis=0, tiled=True),
        lax.all_gather(shards[1], ("seq", "fsdp"), axis=0, tiled=True),
        lax.all_gather(shards[2], ("seq", "fsdp"), axis=0, tiled=True),
        lax.all_gather(shards[3], ("seq", "fsdp"), axis=0, tiled=True),
        lax.all_gather(shards[4], ("seq", "fsdp"), axis=0, tiled=True),
        lax.all_gather(shards[5], ("seq", "fsdp"), axis=0, tiled=True),
        lax.all_gather(shards[6], ("seq", "fsdp"), axis=0, tiled=True),
        lax.all_gather(shards[7], ("seq", "fsdp"), axis=0, tiled=True),
        lax.all_gather(shards[8], ("seq", "fsdp"), axis=0, tiled=True),
        lax.all_gather(shards[9], ("seq", "fsdp"), axis=0, tiled=True),
    )
    batches, positions, width = tokens.shape
    head_count = w_beta.shape[1]
    key_dim = w_query.shape[1]
    value_dim = value_weight.shape[1]
    ff_width = w_mlp_gate.shape[1]
    head_k = key_dim // head_count
    head_v = value_dim // head_count
    row_count = batches * positions
    whq, whk, whv, whg, whb, wha, who, whm, whu, whd = gathered
    flattened = tokens.reshape(row_count, width).astype(jnp.float32)
    normed, pull_first = jax.vjp(rms_scale, flattened, attn_gain)
    normed_b = normed.astype(jnp.bfloat16)
    query_b = (
        bf_dot(normed_b, whq).astype(jnp.bfloat16).reshape(batches, positions, head_count, head_k)
    )
    key_b = (
        bf_dot(normed_b, whk).astype(jnp.bfloat16).reshape(batches, positions, head_count, head_k)
    )
    value_b = (
        bf_dot(normed_b, whv).astype(jnp.bfloat16).reshape(batches, positions, head_count, head_v)
    )
    logit_pair = jnp.stack(
        [bf_dot(normed_b, whb).astype(jnp.bfloat16), bf_dot(normed_b, wha).astype(jnp.bfloat16)],
        axis=-1,
    )
    logit_pair = logit_pair.reshape(batches, positions, head_count, 2)
    attn_gate = bf_dot(normed_b, whg)
    moved = (
        lax.all_to_all(query_b, "seq", split_axis=2, concat_axis=1, tiled=True),
        lax.all_to_all(key_b, "seq", split_axis=2, concat_axis=1, tiled=True),
        lax.all_to_all(value_b, "seq", split_axis=2, concat_axis=1, tiled=True),
        lax.all_to_all(logit_pair, "seq", split_axis=2, concat_axis=1, tiled=True),
    )
    local = head_count // lax.axis_size("seq")
    first = lax.axis_index("seq") * local
    conv_q_local = lax.dynamic_slice_in_dim(conv_query, first * head_k, local * head_k, 1)
    conv_k_local = lax.dynamic_slice_in_dim(conv_key, first * head_k, local * head_k, 1)
    conv_v_local = lax.dynamic_slice_in_dim(conv_value, first * head_v, local * head_v, 1)
    rate_local = lax.dynamic_slice_in_dim(decay_rate, first, local, 0)
    bias_local = lax.dynamic_slice_in_dim(decay_bias, first, local, 0)
    mixed, pull_heads = jax.vjp(
        head_piece,
        moved[0].astype(jnp.float32),
        moved[1].astype(jnp.float32),
        moved[2].astype(jnp.float32),
        moved[3].astype(jnp.float32),
        conv_q_local,
        conv_k_local,
        conv_v_local,
        rate_local,
        bias_local,
    )
    returned = lax.all_to_all(
        mixed.astype(jnp.bfloat16), "seq", split_axis=1, concat_axis=2, tiled=True
    )
    gate_heads = attn_gate.reshape(row_count, head_count, head_v)
    normed_out, pull_out = jax.vjp(
        out_piece,
        returned.reshape(row_count, head_count, head_v).astype(jnp.float32),
        gate_heads,
        out_gain,
    )
    normed_out_b = normed_out.reshape(row_count, value_dim).astype(jnp.bfloat16)
    hidden = flattened + bf_dot(normed_out_b, who)
    normed2, pull_second = jax.vjp(rms_scale, hidden, mlp_gain)
    normed2_b = normed2.astype(jnp.bfloat16)
    mlp_gate = bf_dot(normed2_b, whm)
    up_values = bf_dot(normed2_b, whu)
    mid, pull_mid = jax.vjp(swish_piece, mlp_gate, up_values)
    mid_b = mid.astype(jnp.bfloat16)
    result = (hidden + bf_dot(mid_b, whd)).astype(jnp.bfloat16).reshape(tokens.shape)
    whq, whk, whv, whg, whb, wha, who, whm, whu, whd = gathered
    grad_out_b = cotangent.reshape(row_count, width)
    grad_out = grad_out_b.astype(jnp.float32)
    grad_mid = bf_dot(grad_out_b, whd.T)
    grad_gate_m, grad_up_m = pull_mid(grad_mid)
    grad_gate_mb = grad_gate_m.astype(jnp.bfloat16)
    grad_up_mb = grad_up_m.astype(jnp.bfloat16)
    grad_normed2 = bf_dot(grad_gate_mb, whm.T) + bf_dot(grad_up_mb, whu.T)
    grad_hidden_part, grad_mlp_gain = pull_second(grad_normed2)
    grad_hidden = grad_out + grad_hidden_part
    grad_hidden_b = grad_hidden.astype(jnp.bfloat16)
    grad_normed_out = bf_dot(grad_hidden_b, who.T).reshape(row_count, head_count, head_v)
    grad_returned, grad_gate_heads, grad_out_gain = pull_out(grad_normed_out)
    ffn_grads = jnp.concatenate([grad_gate_mb, grad_up_mb], axis=1)
    grad_mixed = lax.all_to_all(
        grad_returned.astype(jnp.bfloat16).reshape(batches, positions, head_count, head_v),
        "seq",
        split_axis=2,
        concat_axis=1,
        tiled=True,
    )
    head_grads = pull_heads(grad_mixed.astype(jnp.float32))
    grad_q, grad_k, grad_v, grad_pair, grad_cq, grad_ck, grad_cv, grad_rate, bias_gradient = (
        head_grads
    )
    sent_back = (
        lax.all_to_all(grad_q.astype(jnp.bfloat16), "seq", split_axis=1, concat_axis=2, tiled=True),
        lax.all_to_all(grad_k.astype(jnp.bfloat16), "seq", split_axis=1, concat_axis=2, tiled=True),
        lax.all_to_all(grad_v.astype(jnp.bfloat16), "seq", split_axis=1, concat_axis=2, tiled=True),
        lax.all_to_all(
            grad_pair.astype(jnp.bfloat16), "seq", split_axis=1, concat_axis=2, tiled=True
        ),
    )
    back_q = sent_back[0].reshape(row_count, key_dim)
    back_k = sent_back[1].reshape(row_count, key_dim)
    back_v = sent_back[2].reshape(row_count, value_dim)
    back_pair = sent_back[3].reshape(row_count, head_count, 2)
    back_beta = back_pair[:, :, 0]
    back_decay = back_pair[:, :, 1]
    grad_gate_b = grad_gate_heads.reshape(row_count, value_dim).astype(jnp.bfloat16)
    normed_gradient = (
        bf_dot(back_q, whq.T)
        + bf_dot(back_k, whk.T)
        + bf_dot(back_v, whv.T)
        + bf_dot(grad_gate_b, whg.T)
        + bf_dot(back_beta, whb.T)
        + bf_dot(back_decay, wha.T)
    )
    grad_flat, grad_attn_gain = pull_first(normed_gradient)
    grad_tokens = (grad_flat + grad_hidden).reshape(tokens.shape)
    mixer_grads = jnp.concatenate(
        [back_q, back_k, back_v, grad_gate_b, back_beta, back_decay], axis=1
    )
    mixer_sum = lax.psum_scatter(
        column_term(normed_b, mixer_grads), ("seq", "fsdp"), scatter_dimension=0, tiled=True
    )
    ffn_sum = lax.psum_scatter(
        column_term(normed2_b, ffn_grads), ("seq", "fsdp"), scatter_dimension=0, tiled=True
    )
    out_sum = lax.psum_scatter(
        column_term(normed_out_b, grad_hidden_b), ("seq", "fsdp"), scatter_dimension=0, tiled=True
    )
    down_sum = lax.psum_scatter(
        column_term(mid_b, grad_out_b), ("seq", "fsdp"), scatter_dimension=0, tiled=True
    )
    later_sums = (ffn_sum, out_sum, down_sum)
    ffn_sum, out_sum, down_sum = later_sums
    small = lax.psum(
        (
            grad_attn_gain,
            grad_out_gain,
            grad_mlp_gain,
            widen(grad_cq, conv_query.shape, first * head_k),
            widen(grad_ck, conv_key.shape, first * head_k),
            widen(grad_cv, conv_value.shape, first * head_v),
            widen(grad_rate, decay_rate.shape, first),
            widen(bias_gradient, decay_bias.shape, first),
        ),
        ("seq", "fsdp"),
    )
    sum_attn, sum_out_gain, sum_mlp_gain, sum_cq, sum_ck, sum_cv, sum_rate, sum_bias = small
    edge_two = 2 * key_dim
    edge_three = edge_two + value_dim
    edge_four = edge_three + value_dim
    edge_five = edge_four + head_count
    sum_wq = mixer_sum[:, :key_dim]
    sum_wk = mixer_sum[:, key_dim:edge_two]
    sum_wv = mixer_sum[:, edge_two:edge_three]
    sum_wg = mixer_sum[:, edge_three:edge_four]
    sum_wb = mixer_sum[:, edge_four:edge_five]
    sum_wa = mixer_sum[:, edge_five:]
    sum_wm = ffn_sum[:, :ff_width]
    sum_wu = ffn_sum[:, ff_width:]
    return (
        result,
        grad_tokens,
        sum_attn,
        sum_wq,
        sum_wk,
        sum_wv,
        sum_wg,
        sum_wb,
        sum_wa,
        sum_cq,
        sum_ck,
        sum_cv,
        sum_rate,
        sum_bias,
        sum_out_gain,
        out_sum,
        sum_mlp_gain,
        sum_wm,
        sum_wu,
        down_sum,
    )


def solution(mesh):
    in_specs = (
        P("fsdp", "seq", None),
        P(),
        P(("seq", "fsdp"), None),
        P(("seq", "fsdp"), None),
        P(("seq", "fsdp"), None),
        P(("seq", "fsdp"), None),
        P(("seq", "fsdp"), None),
        P(("seq", "fsdp"), None),
        P(),
        P(),
        P(),
        P(),
        P(),
        P(),
        P(("seq", "fsdp"), None),
        P(),
        P(("seq", "fsdp"), None),
        P(("seq", "fsdp"), None),
        P(("seq", "fsdp"), None),
        P("fsdp", "seq", None),
    )
    out_specs = (
        P("fsdp", "seq", None),
        P("fsdp", "seq", None),
        P(),
        P(("seq", "fsdp"), None),
        P(("seq", "fsdp"), None),
        P(("seq", "fsdp"), None),
        P(("seq", "fsdp"), None),
        P(("seq", "fsdp"), None),
        P(("seq", "fsdp"), None),
        P(),
        P(),
        P(),
        P(),
        P(),
        P(),
        P(("seq", "fsdp"), None),
        P(),
        P(("seq", "fsdp"), None),
        P(("seq", "fsdp"), None),
        P(("seq", "fsdp"), None),
    )
    return jax.shard_map(
        on_device, mesh=mesh, in_specs=in_specs, out_specs=out_specs, check_vma=False
    )
```

profile of v0, /device:TPU:0, one launch (start us, length us, event | category | flops | bytes accessed | tf_op | source)
XLA Modules:
  0.0 1610.2 jit_solution(16786233668338584768)
XLA Ops:
  11.9 43.7 %all-gather.1 = bf16[32,32,8]{1,2,0:T(8,128)(2,1)S(1)} all-gather(bf16[1,32,8]{1,2,0:T(8,128)(2,1)} %bitcast.701), channel_id=1, replica_groups=mesh['seq'=4,'fsdp'=8] {'seq','fsdp'}, dimensions={0}, use_global_device_ids=true | all-gather | bytes 16896 | tf_op jit(solution)/shard_map/all_gather | solution.py:172
  55.8 37.2 %all-gather = bf16[32,32,8]{1,2,0:T(8,128)(2,1)S(1)} all-gather(bf16[1,32,8]{1,2,0:T(8,128)(2,1)} %bitcast.702), channel_id=1, replica_groups=mesh['seq'=4,'fsdp'=8] {'seq','fsdp'}, dimensions={0}, use_global_device_ids=true | all-gather | bytes 16896 | tf_op jit(solution)/shard_map/all_gather | solution.py:171
  96.4 3.2 all-to-all-start
  109.3 3.4 all-to-all-start.1
  112.7 17.0 %all-gather.15.cloned.1.call-done = bf16[1024,1024]{1,0:T(8,128)(2,1)} async-done(((bf16[32,1024]{1,0:T(8,128)(2,1)}), bf16[1024,1024]{1,0:T(8,128)(2,1)}) %all-gather.15.cloned.1.call-update) | async-done | bytes 2097168 | tf_op jit(solution)/shard_map/all_gather | solution.py:167
  132.6 3.4 all-to-all-start.3
  139.7 2.3 all-to-all-done.3
  145.8 47.4 %all-gather.13.cloned.1.call-done = bf16[1024,2048]{1,0:T(8,128)(2,1)} async-done(((bf16[32,2048]{1,0:T(8,128)(2,1)}), bf16[1024,2048]{1,0:T(8,128)(2,1)}) %all-gather.13.cloned.1.call-update) | async-done | bytes 4194320 | tf_op jit(solution)/shard_map/all_gather | solution.py:169
  193.2 3.0 convolution_convert_fusion
  197.2 15.0 all-to-all-start.2
  213.3 7.3 all-to-all-done.2
  222.0 2.3 copy.477
  226.3 159.2 %while.44 = (s32[]{:T(128)}, f32[2,128,256]{2,1,0:T(8,128)S(1)}, bf16[8,2,64,256]{3,2,0,1:T(8,128)(2,1)}, f32[8,2,128,256]{3,2,1,0:T(8,128)}, f32[8,2,64]{2,1,0:...) while((s32[]{:T(128)}, f32[2,128,256]{2,1,0:T(8,128)S(1)}, ...), condition=%wide.region_5.7_spmd.clone.clone, body=%wide.region_3.6_spmd.clone.clone.sunk | while | flops 239825088 | bytes 3950322 | solution.py:79
  232.3 9.8 custom-call.28
  252.2 9.8 custom-call.28
  272.1 9.9 custom-call.28
  292.0 9.9 custom-call.28
  311.9 9.8 custom-call.28
  331.8 9.8 custom-call.28
  351.7 9.8 custom-call.28
  371.6 9.8 custom-call.28
  385.5 2.8 copy.493
  388.2 3.5 all-to-all-start.4
  391.8 6.4 copy.497
  401.7 4.8 multiply_convert_fusion.2
  406.9 3.2 multiply_reduce_fusion.22
  410.2 4.8 fusion.217
  415.0 45.8 %all-gather.23.cloned.1.call-done = bf16[1024,2816]{1,0:T(8,128)(2,1)} async-done(((bf16[32,2816]{1,0:T(8,128)(2,1)}), bf16[1024,2816]{1,0:T(8,128)(2,1)}) %all-gather.23.cloned.1.call-update) | async-done | bytes 5767184 | tf_op jit(solution)/shard_map/all_gather | solution.py:175
  460.8 4.7 fusion.218
  465.5 64.4 %all-gather.25.cloned.1.call-done = bf16[2816,1024]{1,0:T(8,128)(2,1)} async-done(((bf16[88,1024]{1,0:T(8,128)(2,1)}), bf16[2816,1024]{1,0:T(8,128)(2,1)}) %all-gather.25.cloned.1.call-update) | async-done | bytes 5767184 | tf_op jit(solution)/shard_map/all_gather | solution.py:176
  529.9 6.6 multiply_convert_fusion
  536.6 5.2 fusion.219
  541.8 2.6 multiply_reduce_fusion.12
  546.9 2.6 copy.500
  549.5 3.8 multiply_reduce_fusion.6
  554.7 3.5 all-to-all-start.5
  558.7 10.7 fusion.118
  574.6 233.2 %while.43 = (s32[]{:T(128)}, f32[2,128,256]{2,1,0:T(8,128)}, f32[8,2,64,128]{3,2,0,1:T(8,128)}, f32[8,2,64,128]{3,2,0,1:T(8,128)}, f32[8,2,64,256]{3,2,0,1:T(8,1...) while((s32[]{:T(128)}, f32[2,128,256]{2,1,0:T(8,128)}, ...), condition=%wide.region_22.24_spmd.clone, body=%wide.region_10.23_spmd.clone.sunk | while | flops 649626816 | bytes 11436403 | solution.py:79
  582.1 9.8 custom-call.27
  611.4 9.8 custom-call.27
  640.6 9.8 custom-call.27
  669.9 9.8 custom-call.27
  699.2 9.8 custom-call.27
  728.4 9.8 custom-call.27
  757.7 9.8 custom-call.27
  787.0 9.8 custom-call.27
  807.9 2.6 copy.627
  814.1 4.1 all-to-all-start.9
  825.7 4.2 all-to-all-start.6
  831.3 3.9 all-to-all-done.6
  835.2 3.4 all-to-all-start.7
  841.1 2.9 all-to-all-done.7
  844.0 3.5 all-to-all-start.8
  850.4 3.6 all-to-all-done.8
  857.2 11.8 fusion.196
  869.8 2.6 fusion.220
  872.4 2.4 convolution_add_fusion.14
  879.9 4.5 fusion.178
  885.6 6.0 fusion.171
  891.6 4.3 fusion.126
  898.9 248.6 %reduce-scatter.5.cloned.1.call-done = f32[32,6160]{1,0:T(8,128)} async-done(((f32[1024,6160]{1,0:T(8,128)}), f32[32,6160]{1,0:T(8,128)}) %reduce-scatter.5.cloned.1.call-update) | async-done | bytes 788496 | tf_op jit(solution)/shard_map/reduce_scatter | solution.py:302
  1153.3 122.4 %all-reduce.36.cloned.1.call-done = (f32[1024]{0:T(1024)}, f32[4,1024]{1,0:T(4,128)}, f32[4,1024]{1,0:T(4,128)}, f32[4,2048]{1,0:T(4,128)}, f32[8]{0:T(128)}, /*index=5*/f32[8]{0:T(128)}, f32[256]{0:T(256)}, f32[1024]{0:T(1024)}) async-done(((f32[1024]{0:T(1024)}, f32[4,1024]{1,0:T(4,128)}, f32[4,1024]{1,0:T(4,128)}, f32[4,2048]{1,0:T(4,128)}, f32[8]{0:T(128)}, /*index=5*/f32[8]{0:T(128)}, f32[256]{0:T(256)}, ...) | async-done | bytes 74832 | tf_op jit(solution)/shard_map/psum | solution.py:316
  1275.6 156.7 %reduce-scatter.7.cloned.1.call-done = f32[64,1024]{1,0:T(8,128)} async-done(((f32[2048,1024]{1,0:T(8,128)}), f32[64,1024]{1,0:T(8,128)}) %reduce-scatter.7.cloned.1.call-update) | async-done | bytes 262160 | tf_op jit(solution)/shard_map/reduce_scatter | solution.py:308
  1432.3 161.1 %reduce-scatter.11.cloned.1.call-done = f32[88,1024]{1,0:T(8,128)} async-done(((f32[2816,1024]{1,0:T(8,128)}), f32[88,1024]{1,0:T(8,128)}) %reduce-scatter.11.cloned.1.call-update) | async-done | bytes 360464 | tf_op jit(solution)/shard_map/reduce_scatter | solution.py:311
  (887 shorter events, 325.9 us)
Async XLA Ops:
  7.2 88.3 %copy-start.1 = (bf16[1,128,1024]{2,1,0:T(8,128)(2,1)S(1)}, bf16[1,128,1024]{2,1,0:T(8,128)(2,1)}, u32[]{:S(2)}) copy-start(bf16[1,128,1024]{2,1,0:T(8,128)(2,1)} %param.26) | copy-start | bytes 786436
  7.2 88.4 %copy-start.37 = (f32[1024]{0:T(1024)S(1)}, f32[1024]{0:T(1024)}, u32[]{:S(2)}) copy-start(f32[1024]{0:T(1024)} %param.27) | copy-start | bytes 12292
  7.2 96.1 %copy-start.90 = (f32[8]{0:T(128)S(1)}, f32[8]{0:T(128)}, u32[]{:S(2)}) copy-start(f32[8]{0:T(128)} %param.37) | copy-start | bytes 100
  7.2 96.2 %copy-start.91 = (f32[8]{0:T(128)S(1)}, f32[8]{0:T(128)}, u32[]{:S(2)}) copy-start(f32[8]{0:T(128)} %param.38) | copy-start | bytes 100
  7.2 99.2 %all-gather.11.cloned.1.call-start = ((), (), s32[]{:S(2)}) async-start(), calls=%async_computation.14 | async-start | bytes 2162688 | tf_op jit(solution)/shard_map/all_gather | solution.py:168
  8.0 121.7 %all-gather.15.cloned.1.call-start = ((), (), s32[]{:S(2)}) async-start(), calls=%async_computation.16 | async-start | bytes 2162688 | tf_op jit(solution)/shard_map/all_gather | solution.py:167
  8.7 184.5 %all-gather.13.cloned.1.call-start = ((), (), s32[]{:S(2)}) async-start(), calls=%async_computation.15 | async-start | bytes 4325376 | tf_op jit(solution)/shard_map/all_gather | solution.py:169
  9.5 382.3 %all-gather.17.cloned.1.call-start = ((), (), s32[]{:S(2)}) async-start(), calls=%async_computation.17 | async-start | bytes 4325376 | tf_op jit(solution)/shard_map/all_gather | solution.py:170
  10.0 396.8 %all-gather.19.cloned.1.call-start = ((), (), s32[]{:S(2)}) async-start(), calls=%async_computation.18 | async-start | bytes 4325376 | tf_op jit(solution)/shard_map/all_gather | solution.py:173
  10.6 399.6 %all-gather.21.cloned.1.call-start = ((), (), s32[]{:S(2)}) async-start(), calls=%async_computation.19 | async-start | bytes 5947392 | tf_op jit(solution)/shard_map/all_gather | solution.py:174
  11.2 449.6 %all-gather.23.cloned.1.call-start = ((), (), s32[]{:S(2)}) async-start(), calls=%async_computation.20 | async-start | bytes 5947392 | tf_op jit(solution)/shard_map/all_gather | solution.py:175
  94.3 307.4 %copy-start.52 = (f32[128]{0:T(128)}, f32[128]{0:T(128)S(1)}, u32[]{:S(2)}) copy-start(f32[128]{0:T(128)S(1)} %fusion.191) | copy-start | bytes 1540
  96.4 7.9 all-to-all-start
  99.7 430.2 %all-gather.25.cloned.1.call-start = ((), (), s32[]{:S(2)}) async-start(), calls=%async_computation.21 | async-start | bytes 5947392 | tf_op jit(solution)/shard_map/all_gather | solution.py:176
  102.3 122.1 %copy-start.54 = (f32[1,512]{1,0:T(1,128)}, f32[1,512]{1,0:T(1,128)S(1)}, u32[]{:S(2)}) copy-start(f32[1,512]{1,0:T(1,128)S(1)} %get-tuple-element.1031) | copy-start | bytes 6148
  102.3 122.1 %copy-start.56 = (f32[1,512]{1,0:T(1,128)}, f32[1,512]{1,0:T(1,128)S(1)}, u32[]{:S(2)}) copy-start(f32[1,512]{1,0:T(1,128)S(1)} %get-tuple-element.1032) | copy-start | bytes 6148
  102.3 122.1 %copy-start.58 = (f32[1,512]{1,0:T(1,128)}, f32[1,512]{1,0:T(1,128)S(1)}, u32[]{:S(2)}) copy-start(f32[1,512]{1,0:T(1,128)S(1)} %get-tuple-element.1033) | copy-start | bytes 6148
  102.3 122.1 %copy-start.60 = (f32[1,512]{1,0:T(1,128)}, f32[1,512]{1,0:T(1,128)S(1)}, u32[]{:S(2)}) copy-start(f32[1,512]{1,0:T(1,128)S(1)} %get-tuple-element.1034) | copy-start | bytes 6148
  103.3 34.0 %copy-start.64 = (f32[1,256]{1,0:T(1,128)}, f32[1,256]{1,0:T(1,128)S(1)}, u32[]{:S(2)}) copy-start(f32[1,256]{1,0:T(1,128)S(1)} %get-tuple-element.1039) | copy-start | bytes 3076
  103.3 34.0 %copy-start.66 = (f32[1,256]{1,0:T(1,128)}, f32[1,256]{1,0:T(1,128)S(1)}, u32[]{:S(2)}) copy-start(f32[1,256]{1,0:T(1,128)S(1)} %get-tuple-element.1040) | copy-start | bytes 3076
  103.3 34.0 %copy-start.68 = (f32[1,256]{1,0:T(1,128)}, f32[1,256]{1,0:T(1,128)S(1)}, u32[]{:S(2)}) copy-start(f32[1,256]{1,0:T(1,128)S(1)} %get-tuple-element.1041) | copy-start | bytes 3076
  103.3 33.9 %copy-start.70 = (f32[1,256]{1,0:T(1,128)}, f32[1,256]{1,0:T(1,128)S(1)}, u32[]{:S(2)}) copy-start(f32[1,256]{1,0:T(1,128)S(1)} %get-tuple-element.1042) | copy-start | bytes 3076
  103.3 39.2 %copy-start.72 = (f32[1,256]{1,0:T(1,128)}, f32[1,256]{1,0:T(1,128)S(1)}, u32[]{:S(2)}) copy-start(f32[1,256]{1,0:T(1,128)S(1)} %get-tuple-element.1054) | copy-start | bytes 3076
  103.3 39.2 %copy-start.74 = (f32[1,256]{1,0:T(1,128)}, f32[1,256]{1,0:T(1,128)S(1)}, u32[]{:S(2)}) copy-start(f32[1,256]{1,0:T(1,128)S(1)} %get-tuple-element.1055) | copy-start | bytes 3076
  103.4 39.2 %copy-start.76 = (f32[1,256]{1,0:T(1,128)}, f32[1,256]{1,0:T(1,128)S(1)}, u32[]{:S(2)}) copy-start(f32[1,256]{1,0:T(1,128)S(1)} %get-tuple-element.1056) | copy-start | bytes 3076
  103.4 39.2 %copy-start.78 = (f32[1,256]{1,0:T(1,128)}, f32[1,256]{1,0:T(1,128)S(1)}, u32[]{:S(2)}) copy-start(f32[1,256]{1,0:T(1,128)S(1)} %get-tuple-element.1057) | copy-start | bytes 3076
  109.3 23.3 %all-to-all-start.1 = ((bf16[1,128,8,128]{3,1,0,2:T(8,128)(2,1)}), bf16[1,128,8,128]{3,1,0,2:T(8,128)(2,1)S(1)}, u32[]{:S(2)}, u32[]{:S(2)}) async-start(bf16[1,128,8,128]{3,1,0,2:T(8,128)(2,1)} %copy.467), calls=%async_computation.1 | async-start | bytes 524288 | tf_op jit(solution)/shard_map/all_to_all | solution.py:207
  132.6 9.4 all-to-all-start.3
  142.5 53.6 %copy-start.19 = (f32[1,512,256]{2,1,0:T(8,128)}, f32[1,512,256]{2,1,0:T(8,128)S(1)}, u32[]{:S(2)}) copy-start(f32[1,512,256]{2,1,0:T(8,128)S(1)} %copy.483) | copy-start | bytes 1572868
  145.8 66.4 %copy-start.48 = (f32[512,2]{0,1:T(2,128)}, f32[512,2]{0,1:T(2,128)S(1)}, u32[]{:S(2)}) copy-start(f32[512,2]{0,1:T(2,128)S(1)} %copy.485) | copy-start | bytes 12292
  197.2 23.4 %all-to-all-start.2 = ((bf16[1,128,8,256]{3,1,0,2:T(8,128)(2,1)}), bf16[1,128,8,256]{3,1,0,2:T(8,128)(2,1)S(1)}, u32[]{:S(2)}, u32[]{:S(2)}) async-start(bf16[1,128,8,256]{3,1,0,2:T(8,128)(2,1)} %copy.474), calls=%async_computation.2 | async-start | bytes 1048576 | tf_op jit(solution)/shard_map/all_to_all | solution.py:208
  385.5 12.7 copy-start.14
  388.2 11.4 all-to-all-start.4
  410.2 50.6 %copy-start.10 = (bf16[128,1024]{1,0:T(8,128)(2,1)}, bf16[128,1024]{1,0:T(8,128)(2,1)S(1)}, u32[]{:S(2)}) copy-start(bf16[128,1024]{1,0:T(8,128)(2,1)S(1)} %multiply_convert_fusion.3) | copy-start | bytes 786436
  415.0 114.9 %copy-start.34 = (bf16[1,128,1024]{2,1,0:T(8,128)(2,1)S(1)}, bf16[1,128,1024]{2,1,0:T(8,128)(2,1)}, u32[]{:S(2)}) copy-start(bf16[1,128,1024]{2,1,0:T(8,128)(2,1)} %param.45) | copy-start | bytes 786436
  554.7 14.7 all-to-all-start.5
  558.2 338.7 %reduce-scatter.9.cloned.1.call-start = ((), (), s32[]{:S(2)}) async-start(), calls=%async_computation.24 | async-start | bytes 23789568 | tf_op jit(solution)/shard_map/reduce_scatter | solution.py:305
  807.8 11.6 copy-start.25
  807.8 11.9 copy-start.47
  807.8 11.9 copy-start.49
  807.8 11.9 copy-start.20
  807.8 11.9 copy-start.24
  814.1 11.6 all-to-all-start.9
  824.4 5.4 copy-start.65
  824.5 5.4 copy-start.67
  824.5 5.4 copy-start.69
  824.5 5.4 copy-start.71
  825.7 9.6 all-to-all-start.6
  830.1 8.6 copy-start.55
  830.1 8.6 copy-start.57
  830.1 8.6 copy-start.59
  830.1 8.6 copy-start.61
  835.2 8.8 all-to-all-start.7
  839.8 7.7 copy-start.33
  844.0 10.0 all-to-all-start.8
  847.5 300.1 %reduce-scatter.5.cloned.1.call-start = ((), (), s32[]{:S(2)}) async-start(), calls=%async_computation.22 | async-start | bytes 26492928 | tf_op jit(solution)/shard_map/reduce_scatter | solution.py:302
  850.4 6.8 copy-start.53
  869.1 406.6 %all-reduce.36.cloned.1.call-start = ((), (), s32[]{:S(2)}) async-start(), calls=%async_computation.26 | async-start | bytes 151552 | tf_op jit(solution)/shard_map/psum | solution.py:316
  869.4 5.4 copy-start.88
  869.4 5.4 copy-start.40
  869.5 5.4 copy-start.39
  869.5 5.3 copy-start.38
  879.9 552.5 %reduce-scatter.7.cloned.1.call-start = ((), (), s32[]{:S(2)}) async-start(), calls=%async_computation.23 | async-start | bytes 8650752 | tf_op jit(solution)/shard_map/reduce_scatter | solution.py:308
  884.4 709.0 %reduce-scatter.11.cloned.1.call-start = ((), (), s32[]{:S(2)}) async-start(), calls=%async_computation.25 | async-start | bytes 11894784 | tf_op jit(solution)/shard_map/reduce_scatter | solution.py:311
  (51 other events, 128.6 us)
Sparse Core Ops, SparseCore 0:
  11.1 59.2 all-gather.10
  73.4 56.2 all-gather.14
  132.7 60.4 all-gather.12
  196.0 60.8 all-gather.16
  259.8 62.0 all-gather.18
  324.6 66.9 all-gather.20
  394.4 66.3 all-gather.22
  463.7 66.2 all-gather.24
  569.5 252.3 reduce-scatter.8
  869.2 278.2 reduce-scatter.4
  1156.8 118.7 all-reduce.35
  1278.4 153.9 reduce-scatter.6
  1435.2 158.1 reduce-scatter.10
where the time goes:
time: 1620 us; the launch traced here: 1610 us
  waiting for transfers between devices  891 us (55%)
  other arithmetic  232 us (14%)
  matrix products  216 us (13%)
  local copies, waits for them, and re-layouts  124 us (8%)
  blocking collectives  81 us (5%)
  starting transfers between devices  48.3 us (3%)
    reduce_scatter x1, waiting for transfers between devices, on_device(): lax.psum_scatter(column_term(normed_b, mixer_grads), ('seq', 'fsdp'), sca...  249 us
    reduce_scatter x1, waiting for transfers between devices, on_device(): lax.psum_scatter(column_term(mid_b, grad_out_b), ('seq', 'fsdp'), scatter...  161 us
    another operation x56, other arithmetic, block_step(): jax.scipy.linalg.solve_triangular(system, right_side, lower=True, unit_di...  160 us
    reduce_scatter x1, waiting for transfers between devices, on_device(): lax.psum_scatter(column_term(normed_out_b, grad_hidden_b), ('seq', 'fsdp'...  157 us
    psum x1, waiting for transfers between devices, on_device(): lax.psum((grad_attn_gain, grad_out_gain, grad_mlp_gain, widen(grad_cq, co...  122 us
    dot_general x176, matrix products, product(): return jnp.dot(left, right, precision=highest_precision)  112 us
    dot_general x24, matrix products, bf_dot(): return jnp.dot(left, right, preferred_element_type=jnp.float32)  89.3 us
    all_gather x1, waiting for transfers between devices, on_device(): lax.all_gather(shards[9], ('seq', 'fsdp'), axis=0, tiled=True)  64.4 us
  transfers between devices with their start and end apart: 23, of which 15 were waited for; matrix products, arithmetic and copies ran while one was open for 33% of the time, Pallas kernels for 0%

commit v1 on v0

v1 whole, which is shorter than its diff:
```python
import jax
import jax.numpy as jnp
from jax import lax
from jax.experimental import pallas as pl
from jax.experimental.pallas import tpu as pltpu
from jax.sharding import PartitionSpec as P

CHUNK = 128


epsilon = 1e-06
highest_precision = lax.Precision.HIGHEST


def bf_dot(left, right):
    return jnp.dot(left, right, preferred_element_type=jnp.float32)


def rms_scale(signal, gain):
    return signal * lax.rsqrt(jnp.mean(signal * signal, axis=-1, keepdims=True) + epsilon) * gain


def unit_rows(signal):
    return signal * lax.rsqrt(jnp.sum(signal * signal, axis=-1, keepdims=True) + epsilon)


def contract(left, right, left_dim, right_dim):
    return lax.dot_general(
        left,
        right,
        (((left_dim,), (right_dim,)), ((), ())),
        precision=highest_precision,
        preferred_element_type=jnp.float32,
    )


@jax.custom_vjp
def mm(left, right):
    return contract(left, right, 1, 0)


@jax.custom_vjp
def mm_nt(left, right):
    return contract(left, right, 1, 1)


@jax.custom_vjp
def mm_tn(left, right):
    return contract(left, right, 0, 0)


mm.defvjp(
    lambda a, b: (contract(a, b, 1, 0), (a, b)),
    lambda kept, g: (contract(g, kept[1], 1, 1), contract(kept[0], g, 0, 0)),
)
mm_nt.defvjp(
    lambda a, b: (contract(a, b, 1, 1), (a, b)),
    lambda kept, g: (contract(g, kept[1], 1, 0), contract(g, kept[0], 0, 0)),
)
mm_tn.defvjp(
    lambda a, b: (contract(a, b, 0, 0), (a, b)),
    lambda kept, g: (contract(kept[1], g, 1, 1), contract(kept[0], g, 1, 0)),
)


def unit_lower_inverse(lower):
    size = lower.shape[0]
    row = lax.broadcasted_iota(jnp.int32, (size, size), 0)
    col = lax.broadcasted_iota(jnp.int32, (size, size), 1)
    inverse = jnp.where(row == col, 1.0, 0.0).astype(jnp.float32)
    level = 0
    while (1 << level) < size:
        row_block = lax.shift_right_logical(row, level)
        col_block = lax.shift_right_logical(col, level)
        part = jnp.where(
            (row_block == col_block + 1) & (jnp.bitwise_and(row_block, 1) == 1), lower, 0.0
        )
        if level == 0:
            inverse = inverse - part
        else:
            inverse = inverse - contract(contract(inverse, part, 1, 0), inverse, 1, 0)
        level += 1
    return inverse


@jax.custom_vjp
def known_inverse(lower, inverse):
    return inverse


known_inverse.defvjp(
    lambda lower, inverse: (inverse, inverse),
    lambda inverse, g: (
        -contract(contract(inverse, g, 0, 0), inverse, 1, 1),
        jnp.zeros_like(inverse),
    ),
)


def twice(wide, width):
    return jnp.concatenate([wide] * (width // wide.shape[1]), axis=1)


def chunk_step(memory, queries, keys, values, strength, log_decay, inverse=None):
    size = queries.shape[0]
    head_v = values.shape[1]
    row = lax.broadcasted_iota(jnp.int32, (size, size), 0)
    col = lax.broadcasted_iota(jnp.int32, (size, size), 1)
    causal = row >= col
    strict = row > col
    upto = jnp.where(causal, 1.0, 0.0).astype(jnp.float32)
    after = jnp.where(strict, 0.0, 1.0 - jnp.where(row == col, 1.0, 0.0)).astype(jnp.float32)
    pair = jnp.exp(mm(upto, jnp.where(strict, log_decay, 0.0)))
    lower = jnp.where(strict, strength * mm_nt(keys, keys) * pair, 0.0)
    if inverse is None:
        inverse = unit_lower_inverse(lower)
        solve = inverse
    else:
        solve = known_inverse(lower, inverse)
    from_start = jnp.exp(mm(upto, log_decay))
    to_end = jnp.exp(mm(after, log_decay))
    whole = jnp.exp(mm(jnp.ones_like(upto), log_decay))
    right_side = twice(strength, head_v) * values - mm(strength * from_start * keys, memory)
    corrected = mm(solve, right_side)
    scores = jnp.where(causal, mm_nt(queries, keys) * pair, 0.0)
    outputs = mm(from_start * queries, memory) + mm(scores, corrected)
    new_memory = twice(whole, head_v) * memory + mm_tn(keys * to_end, corrected)
    return new_memory, outputs, inverse


def forward_kernel(q_ref, k_ref, v_ref, s_ref, d_ref, out_ref, mem_ref, inv_ref, state):
    @pl.when(pl.program_id(0) == 0)
    def _():
        state[...] = jnp.zeros_like(state)

    for i in range(q_ref.shape[0]):
        memory = state[i]
        mem_ref[0, i] = memory
        new_memory, outputs, inverse = chunk_step(
            memory, q_ref[i], k_ref[i], v_ref[i], s_ref[i], d_ref[i]
        )
        state[i] = new_memory
        out_ref[i] = outputs
        inv_ref[0, i] = inverse


def backward_kernel(
    q_ref, k_ref, v_ref, s_ref, d_ref, mem_ref, inv_ref, g_ref,
    gq_ref, gk_ref, gv_ref, gs_ref, gd_ref, state,
):
    @pl.when(pl.program_id(0) == 0)
    def _():
        state[...] = jnp.zeros_like(state)

    for i in range(q_ref.shape[0]):
        inverse = inv_ref[0, i]

        def step(memory, q, k, v, s, d, inverse=inverse):
            return chunk_step(memory, q, k, v, s, d, inverse)[:2]

        _, pull = jax.vjp(
            step, mem_ref[0, i], q_ref[i], k_ref[i], v_ref[i], s_ref[i], d_ref[i]
        )
        gm, gq, gk, gv, gs, gd = pull((state[i], g_ref[i]))
        state[i] = gm
        gq_ref[i] = gq
        gk_ref[i] = gk
        gv_ref[i] = gv
        gs_ref[i] = gs
        gd_ref[i] = gd


def run_forward(queries, keys, values, strength, log_decay):
    streams, length, head_k = queries.shape
    head_v = values.shape[2]
    chunks = length // CHUNK
    narrow = pl.BlockSpec((streams, CHUNK, head_k), lambda c: (0, c, 0))
    wide = pl.BlockSpec((streams, CHUNK, head_v), lambda c: (0, c, 0))
    memories = pl.BlockSpec((1, streams, head_k, head_v), lambda c: (c, 0, 0, 0))
    inverses = pl.BlockSpec((1, streams, CHUNK, CHUNK), lambda c: (c, 0, 0, 0))
    return pl.pallas_call(
        forward_kernel,
        grid=(chunks,),
        in_specs=[narrow, narrow, wide, narrow, narrow],
        out_specs=[wide, memories, inverses],
        out_shape=[
            jax.ShapeDtypeStruct((streams, length, head_v), jnp.float32),
            jax.ShapeDtypeStruct((chunks, streams, head_k, head_v), jnp.float32),
            jax.ShapeDtypeStruct((chunks, streams, CHUNK, CHUNK), jnp.float32),
        ],
        scratch_shapes=[pltpu.VMEM((streams, head_k, head_v), jnp.float32)],
        compiler_params=pltpu.CompilerParams(vmem_limit_bytes=32 * 1024 * 1024),
        cost_estimate=pl.CostEstimate(
            flops=60_000_000 * chunks * streams, bytes_accessed=8_000_000, transcendentals=0
        ),
        name="recurrence_forward",
    )(queries, keys, values, strength, log_decay)


def run_backward(queries, keys, values, strength, log_decay, memory, inverse, grad):
    streams, length, head_k = queries.shape
    head_v = values.shape[2]
    chunks = length // CHUNK
    last = chunks - 1
    narrow = pl.BlockSpec((streams, CHUNK, head_k), lambda c: (0, last - c, 0))
    wide = pl.BlockSpec((streams, CHUNK, head_v), lambda c: (0, last - c, 0))
    memories = pl.BlockSpec((1, streams, head_k, head_v), lambda c: (last - c, 0, 0, 0))
    inverses = pl.BlockSpec((1, streams, CHUNK, CHUNK), lambda c: (last - c, 0, 0, 0))
    narrow_shape = jax.ShapeDtypeStruct((streams, length, head_k), jnp.float32)
    wide_shape = jax.ShapeDtypeStruct((streams, length, head_v), jnp.float32)
    return pl.pallas_call(
        backward_kernel,
        grid=(chunks,),
        in_specs=[narrow, narrow, wide, narrow, narrow, memories, inverses, wide],
        out_specs=[narrow, narrow, wide, narrow, narrow],
        out_shape=[narrow_shape, narrow_shape, wide_shape, narrow_shape, narrow_shape],
        scratch_shapes=[pltpu.VMEM((streams, head_k, head_v), jnp.float32)],
        compiler_params=pltpu.CompilerParams(vmem_limit_bytes=32 * 1024 * 1024),
        cost_estimate=pl.CostEstimate(
            flops=120_000_000 * chunks * streams, bytes_accessed=12_000_000, transcendentals=0
        ),
        name="recurrence_backward",
    )(queries, keys, values, strength, log_decay, memory, inverse, grad)


def prepare(moved, conv_q, conv_k, conv_v, rate, bias):
    batches, local, length, _ = moved.shape
    head_k = conv_q.shape[2]
    head_v = conv_v.shape[2]

    def conv(signal, kernel):
        taps = kernel.shape[0]
        padded = jnp.pad(signal, [(0, 0), (0, 0), (taps - 1, 0), (0, 0)])
        summed = jnp.zeros_like(signal)
        for offset in range(taps):
            summed = summed + kernel[offset][:, None, :] * lax.slice_in_dim(
                padded, offset, offset + length, axis=2
            )
        return summed

    edge = 2 * head_k + head_v
    queries = unit_rows(jax.nn.silu(conv(moved[..., :head_k], conv_q))) * head_k ** (-0.5)
    keys = unit_rows(jax.nn.silu(conv(moved[..., head_k : 2 * head_k], conv_k)))
    values = jax.nn.silu(conv(moved[..., 2 * head_k : edge], conv_v))
    strength = jax.nn.sigmoid(moved[..., edge : edge + 1])
    log_decay = -rate[:, None, None] * jax.nn.softplus(
        moved[..., edge + 1 : edge + 2] + bias[:, None, None]
    )
    shape = (batches * local, length)
    lanes = (batches, local, length, head_k)
    return (
        queries.reshape(shape + (head_k,)),
        keys.reshape(shape + (head_k,)),
        values.reshape(shape + (head_v,)),
        jnp.broadcast_to(strength, lanes).reshape(shape + (head_k,)),
        jnp.broadcast_to(log_decay, lanes).reshape(shape + (head_k,)),
    )


def to_heads(rows):
    count = lax.axis_size("seq")
    batches, positions, heads, width = rows.shape
    local = heads // count
    split = rows.reshape(batches, positions, count, local, width).transpose(2, 0, 3, 1, 4)
    moved = lax.all_to_all(split, "seq", split_axis=0, concat_axis=0, tiled=True)
    return moved.transpose(1, 2, 0, 3, 4).reshape(batches, local, count * positions, width)


def to_positions(by_head):
    count = lax.axis_size("seq")
    batches, local, length, width = by_head.shape
    positions = length // count
    split = by_head.reshape(batches, local, count, positions, width).transpose(2, 0, 1, 3, 4)
    moved = lax.all_to_all(split, "seq", split_axis=0, concat_axis=0, tiled=True)
    return moved.transpose(1, 3, 0, 2, 4).reshape(batches, positions, count * local, width)


def total_of(vector):
    for axis in ("fsdp", "seq"):
        size = lax.axis_size(axis)
        if size & (size - 1):
            vector = lax.psum(vector, axis)
            continue
        bit = 1
        while bit < size:
            vector = vector + lax.ppermute(vector, axis, [(i, i ^ bit) for i in range(size)])
            bit *= 2
    return vector


def total_small(parts):
    flat = jnp.concatenate([p.reshape(-1) for p in parts])
    count = flat.shape[0]
    padded = -(-count // 1024) * 1024
    summed = total_of(jnp.pad(flat, (0, padded - count)).reshape(-1, 128)).reshape(-1)
    results = []
    start = 0
    for p in parts:
        results.append(summed[start : start + p.size].reshape(p.shape))
        start += p.size
    return results


def gather(shard):
    return lax.all_gather(shard, ("seq", "fsdp"), axis=0, tiled=True)


def scatter(partial):
    return lax.psum_scatter(
        partial.astype(jnp.bfloat16), ("seq", "fsdp"), scatter_dimension=0, tiled=True
    ).astype(jnp.float32)


def out_piece(values, gate_values, gain):
    return rms_scale(values, gain) * jax.nn.silu(gate_values)


def swish_piece(gate_values, up_values):
    return jax.nn.silu(gate_values) * up_values


def widen(part, whole_shape, offset):
    return lax.dynamic_update_slice_in_dim(
        jnp.zeros(whole_shape, jnp.float32), part, offset, part.ndim - 1
    )


def column_term(left, right):
    return bf_dot(left.T, right)


def on_device(
    tokens,
    attn_gain,
    w_query,
    w_key,
    value_weight,
    w_gate,
    w_beta,
    w_decay,
    conv_query,
    conv_key,
    conv_value,
    decay_rate,
    decay_bias,
    out_gain,
    w_out,
    mlp_gain,
    w_mlp_gate,
    w_up,
    w_down,
    cotangent,
):
    batches, positions, width = tokens.shape
    head_count = w_beta.shape[1]
    key_dim = w_query.shape[1]
    value_dim = value_weight.shape[1]
    ff_width = w_mlp_gate.shape[1]
    head_k = key_dim // head_count
    head_v = value_dim // head_count
    row_count = batches * positions
    count = lax.axis_size("seq") * lax.axis_size("fsdp")
    out_rows = w_out.shape[0]
    down_rows = w_down.shape[0]
    edge_two = 2 * key_dim
    edge_three = edge_two + value_dim
    edge_four = edge_three + value_dim
    edge_five = edge_four + head_count
    edge_six = edge_five + head_count

    mixer_w = gather(
        jnp.concatenate([w_query, w_key, value_weight, w_gate, w_beta, w_decay], axis=1)
    )
    ffn_w = gather(jnp.concatenate([w_mlp_gate, w_up], axis=1))
    tall_w = gather(jnp.concatenate([w_out, w_down], axis=0)).reshape(
        count, out_rows + down_rows, width
    )
    who = tall_w[:, :out_rows].reshape(count * out_rows, width)
    whd = tall_w[:, out_rows:].reshape(count * down_rows, width)

    flattened = tokens.reshape(row_count, width).astype(jnp.float32)
    normed, pull_first = jax.vjp(rms_scale, flattened, attn_gain)
    normed_b = normed.astype(jnp.bfloat16)
    projected = bf_dot(normed_b, mixer_w)
    attn_gate = projected[:, edge_three:edge_four]

    def heads_of(columns, size):
        return columns.astype(jnp.bfloat16).reshape(batches, positions, head_count, size)

    logits = jnp.stack([projected[:, edge_four:edge_five], projected[:, edge_five:edge_six]], -1)
    rows = jnp.concatenate(
        [
            heads_of(projected[:, :key_dim], head_k),
            heads_of(projected[:, key_dim:edge_two], head_k),
            heads_of(projected[:, edge_two:edge_three], head_v),
            jnp.pad(heads_of(logits, 2), [(0, 0), (0, 0), (0, 0), (0, 126)]),
        ],
        axis=-1,
    )
    moved = to_heads(rows).astype(jnp.float32)
    local = head_count // lax.axis_size("seq")
    first = lax.axis_index("seq") * local

    def local_taps(kernel, size):
        part = lax.dynamic_slice_in_dim(kernel, first * size, local * size, 1)
        return part.reshape(kernel.shape[0], local, size)

    rate_local = lax.dynamic_slice_in_dim(decay_rate, first, local, 0)
    bias_local = lax.dynamic_slice_in_dim(decay_bias, first, local, 0)
    prepared, pull_prepare = jax.vjp(
        prepare,
        moved,
        local_taps(conv_query, head_k),
        local_taps(conv_key, head_k),
        local_taps(conv_value, head_v),
        rate_local,
        bias_local,
    )
    length = moved.shape[2]
    mixed, memories, inverses = run_forward(*prepared)
    returned = to_positions(
        mixed.astype(jnp.bfloat16).reshape(batches, local, length, head_v)
    )
    gate_heads = attn_gate.reshape(row_count, head_count, head_v)
    normed_out, pull_out = jax.vjp(
        out_piece,
        returned.reshape(row_count, head_count, head_v).astype(jnp.float32),
        gate_heads,
        out_gain,
    )
    normed_out_b = normed_out.reshape(row_count, value_dim).astype(jnp.bfloat16)
    hidden = flattened + bf_dot(normed_out_b, who)
    normed2, pull_second = jax.vjp(rms_scale, hidden, mlp_gain)
    normed2_b = normed2.astype(jnp.bfloat16)
    mlp_both = bf_dot(normed2_b, ffn_w)
    mid, pull_mid = jax.vjp(swish_piece, mlp_both[:, :ff_width], mlp_both[:, ff_width:])
    mid_b = mid.astype(jnp.bfloat16)
    result = (hidden + bf_dot(mid_b, whd)).astype(jnp.bfloat16).reshape(tokens.shape)
    grad_out_b = cotangent.reshape(row_count, width)
    grad_out = grad_out_b.astype(jnp.float32)
    grad_mid = bf_dot(grad_out_b, whd.T)
    grad_gate_m, grad_up_m = pull_mid(grad_mid)
    ffn_grads = jnp.concatenate(
        [grad_gate_m.astype(jnp.bfloat16), grad_up_m.astype(jnp.bfloat16)], axis=1
    )
    grad_normed2 = bf_dot(ffn_grads, ffn_w.T)
    grad_hidden_part, grad_mlp_gain = pull_second(grad_normed2)
    grad_hidden = grad_out + grad_hidden_part
    grad_hidden_b = grad_hidden.astype(jnp.bfloat16)
    grad_normed_out = bf_dot(grad_hidden_b, who.T).reshape(row_count, head_count, head_v)
    grad_returned, grad_gate_heads, grad_out_gain = pull_out(grad_normed_out)
    grad_mixed = to_heads(
        grad_returned.astype(jnp.bfloat16).reshape(batches, positions, head_count, head_v)
    )
    ffn_sum = scatter(column_term(normed2_b, ffn_grads))
    tall_sum = scatter(
        jnp.concatenate(
            [
                column_term(normed_out_b, grad_hidden_b).astype(jnp.bfloat16).reshape(
                    count, out_rows, width
                ),
                column_term(mid_b, grad_out_b).astype(jnp.bfloat16).reshape(
                    count, down_rows, width
                ),
            ],
            axis=1,
        ).reshape(count * (out_rows + down_rows), width)
    )
    prepared_grads = run_backward(
        *prepared,
        memories,
        inverses,
        grad_mixed.astype(jnp.float32).reshape(batches * local, length, head_v),
    )
    grad_moved, grad_cq, grad_ck, grad_cv, grad_rate, bias_gradient = pull_prepare(
        tuple(prepared_grads)
    )
    back = to_positions(grad_moved.astype(jnp.bfloat16)).reshape(row_count, head_count, -1)
    edge = 2 * head_k + head_v
    grad_gate_b = grad_gate_heads.reshape(row_count, value_dim).astype(jnp.bfloat16)
    mixer_grads = jnp.concatenate(
        [
            back[:, :, :head_k].reshape(row_count, key_dim),
            back[:, :, head_k : 2 * head_k].reshape(row_count, key_dim),
            back[:, :, 2 * head_k : edge].reshape(row_count, value_dim),
            grad_gate_b,
            back[:, :, edge],
            back[:, :, edge + 1],
        ],
        axis=1,
    )
    mixer_sum = scatter(column_term(normed_b, mixer_grads))
    normed_gradient = bf_dot(mixer_grads, mixer_w.T)
    grad_flat, grad_attn_gain = pull_first(normed_gradient)
    grad_tokens = (grad_flat + grad_hidden).reshape(tokens.shape)

    def flat_taps(grad):
        return grad.reshape(grad.shape[0], -1)

    small = total_small(
        (
            grad_attn_gain,
            grad_out_gain,
            grad_mlp_gain,
            widen(flat_taps(grad_cq), conv_query.shape, first * head_k),
            widen(flat_taps(grad_ck), conv_key.shape, first * head_k),
            widen(flat_taps(grad_cv), conv_value.shape, first * head_v),
            widen(grad_rate, decay_rate.shape, first),
            widen(bias_gradient, decay_bias.shape, first),
        )
    )
    sum_attn, sum_out_gain, sum_mlp_gain, sum_cq, sum_ck, sum_cv, sum_rate, sum_bias = small
    return (
        result,
        grad_tokens,
        sum_attn,
        mixer_sum[:, :key_dim],
        mixer_sum[:, key_dim:edge_two],
        mixer_sum[:, edge_two:edge_three],
        mixer_sum[:, edge_three:edge_four],
        mixer_sum[:, edge_four:edge_five],
        mixer_sum[:, edge_five:],
        sum_cq,
        sum_ck,
        sum_cv,
        sum_rate,
        sum_bias,
        sum_out_gain,
        tall_sum[:out_rows],
        sum_mlp_gain,
        ffn_sum[:, :ff_width],
        ffn_sum[:, ff_width:],
        tall_sum[out_rows:],
    )


def solution(mesh):
    in_specs = (
        P("fsdp", "seq", None),
        P(),
        P(("seq", "fsdp"), None),
        P(("seq", "fsdp"), None),
        P(("seq", "fsdp"), None),
        P(("seq", "fsdp"), None),
        P(("seq", "fsdp"), None),
        P(("seq", "fsdp"), None),
        P(),
        P(),
        P(),
        P(),
        P(),
        P(),
        P(("seq", "fsdp"), None),
        P(),
        P(("seq", "fsdp"), None),
        P(("seq", "fsdp"), None),
        P(("seq", "fsdp"), None),
        P("fsdp", "seq", None),
    )
    out_specs = (
        P("fsdp", "seq", None),
        P("fsdp", "seq", None),
        P(),
        P(("seq", "fsdp"), None),
        P(("seq", "fsdp"), None),
        P(("seq", "fsdp"), None),
        P(("seq", "fsdp"), None),
        P(("seq", "fsdp"), None),
        P(("seq", "fsdp"), None),
        P(),
        P(),
        P(),
        P(),
        P(),
        P(),
        P(("seq", "fsdp"), None),
        P(),
        P(("seq", "fsdp"), None),
        P(("seq", "fsdp"), None),
        P(("seq", "fsdp"), None),
    )
    return jax.shard_map(
        on_device, mesh=mesh, in_specs=in_specs, out_specs=out_specs, check_vma=False
    )
```

time: 1620 us -> 831 us (0.51)
  waiting for transfers between devices: 891 us -> 552 us
  other arithmetic: 232 us -> 38.2 us
  matrix products: 216 us -> 72.5 us
  blocking collectives: 81 us -> 0 us
  local copies, waits for them, and re-layouts: 124 us -> 61.6 us
  Pallas kernels: 0 us -> 59.7 us
  starting transfers between devices: 48.3 us -> 23.3 us
    reduce_scatter x4 -> x3, waiting for transfers between devices: 566 us -> 313 us  [scatter(): lax.psum_scatter(partial.astype(jnp.bfloat16), ('seq', 'fsdp'), scatter_d...]
    another operation x99 -> x1, other arithmetic: 175 us -> 0.02 us  [on_device(): jnp.stack([projected[:, edge_four:edge_five], projected[:, edge_five:edge...]
    psum x1 -> x0, waiting for transfers between devices: 122 us -> none  [on_device(): lax.psum((grad_attn_gain, grad_out_gain, grad_mlp_gain, widen(grad_cq, co...]
    dot_general x184 -> x0, matrix products: 115 us -> none  [the longest x176 112 us: product(): return jnp.dot(left, right, precision=highest_precision)]
    all_gather x2 -> x0, blocking collectives: 81 us -> none  [the longest x1 43.7 us: on_device(): lax.all_gather(shards[5], ('seq', 'fsdp'), axis=0, tiled=True)]
    pallas_call x0 -> x2, Pallas kernels: none -> 59.7 us  [the longest x1 32.2 us: run_forward(): pl.pallas_call(forward_kernel, grid=(chunks,), in_specs=[narrow, narrow,...]
    squeeze x48 -> x0, local copies, waits for them, and re-layouts: 40.8 us -> none  [delta_blocks(): _, outputs = lax.scan(jax.checkpoint(block_step), memory, shaped)]
    all_to_all x10 -> x4, waiting for transfers between devices: 22.3 us -> 55.2 us  [the longest x2 32 us: to_heads(): lax.all_to_all(split, 'seq', split_axis=0, concat_axis=0, tiled=True)]
  transfers between devices with their start and end apart: 23 -> 15, of which waited for: 15 -> 13; matrix products, arithmetic and copies ran while one was open for 33% -> 15% of each run, Pallas kernels for 0% -> 7%
where the time goes in v1:
time: 831 us; the launch traced here: 823 us
  waiting for transfers between devices  552 us (66%)
  matrix products  72.5 us (9%)
  local copies, waits for them, and re-layouts  61.6 us (7%)
  Pallas kernels  59.7 us (7%)
  other arithmetic  38.2 us (5%)
  starting transfers between devices  23.3 us (3%)
  between operations  15.4 us (2%)
    reduce_scatter x3, waiting for transfers between devices, scatter(): lax.psum_scatter(partial.astype(jnp.bfloat16), ('seq', 'fsdp'), scatter_d...  313 us
    all_gather x3, waiting for transfers between devices, gather(): return lax.all_gather(shard, ('seq', 'fsdp'), axis=0, tiled=True)  172 us
    dot_general x12, matrix products, bf_dot(): return jnp.dot(left, right, preferred_element_type=jnp.float32)  72.5 us
    pallas_call x1, Pallas kernels, run_forward(): pl.pallas_call(forward_kernel, grid=(chunks,), in_specs=[narrow, narrow,...  32.2 us
    all_to_all x2, waiting for transfers between devices, to_heads(): lax.all_to_all(split, 'seq', split_axis=0, concat_axis=0, tiled=True)  32 us
    pallas_call x1, Pallas kernels, run_backward(): pl.pallas_call(backward_kernel, grid=(chunks,), in_specs=[narrow, narrow,...  27.4 us
    all_to_all x2, waiting for transfers between devices, to_positions(): lax.all_to_all(split, 'seq', split_axis=0, concat_axis=0, tiled=True)  23.1 us
  transfers between devices with their start and end apart: 15, of which 13 were waited for; matrix products, arithmetic and copies ran while one was open for 15% of the time, Pallas kernels for 7%

profile of v1, /device:TPU:0, one launch (start us, length us, event | category | flops | bytes accessed | tf_op | source)
XLA Modules:
  0.0 822.8 jit_solution(16819565451946130157)
XLA Ops:
  8.8 1.9 concatenate.41
  10.8 1.7 pad_maximum_fusion.5
  12.6 1.8 pad_maximum_fusion.4
  14.5 97.1 %all-gather.4.cloned.1.call-done = bf16[1024,6160]{1,0:T(8,128)(2,1)} async-done(((bf16[32,6160]{1,0:T(8,128)(2,1)}), bf16[1024,6160]{1,0:T(8,128)(2,1)}) %all-gather.4.cloned.1.call-update) | async-done | bytes 12615696 | tf_op jit(solution)/shard_map/all_gather | solution.py:305
  111.6 11.4 %fusion.82 = (bf16[128,6160]{0,1:T(8,128)(2,1)S(1)}, f32[128,6160]{0,1:T(8,128)}) fusion(bf16[1024,6160]{1,0:T(8,128)(2,1)} %all-gather.4.cloned.1.call-done, bf16[1,128,1024]{2,1,0:T(8,128)(2,1)S(1)} %copy-done.16, f32[1024]{0:T(1024)S(1)} %copy-done.43, f32[128]{0:T(128)S(1)} %fusion.61), kind=kOutput, calls=%fused_computation.227 | convolution fusion | flops 1616119808 | bytes 17613312 | tf_op jit(solution)/shard_map/dot_general | solution.py:16
  124.2 1.1 copy.161
  125.6 1.2 maximum_bitcast_fusion
  126.9 3.8 all-to-all-start
  133.7 19.9 %all-to-all-done = bf16[4,1,2,128,640]{4,3,2,1,0:T(8,128)(2,1)S(1)} async-done(((bf16[4,1,2,128,640]{4,3,2,1,0:T(8,128)(2,1)}), bf16[4,1,2,128,640]{4,3,2,1,0:T(8,128)(2,1)S(1)}, u32[]{:S(2)}, u32[]{:S(2)}) %all-to-all-start) | async-done | bytes 1310752 | tf_op jit(solution)/shard_map/all_to_all | solution.py:265
  156.8 1.6 multiply_bitcast_fusion
  158.8 32.2 %recurrence_forward.1 = (f32[2,512,256]{2,1,0:T(8,128)S(1)}, f32[4,2,128,256]{3,2,1,0:T(8,128)S(1)}, f32[4,2,128,128]{3,2,1,0:T(8,128)S(1)}) custom-call(f32[2,512,128]{2,1,0:T(8,128)S(1)} %multiply_bitcast_fusion.2.q_ref, f32[2,512,128]{2,1,0:T(8,128)S(1)} %multiply_bitcast_fusion.1.k_ref, f32[2,512,256]{2,1,0:T(8,128)S(1)} %get-tuple-element.194.v_ref, ...), custom_call_target="tpu_custom_call" | custom-call | flops 480000000 | bytes 8000000 | tf_op jit(solution)/shard_map/recurrence_forward/pallas_call | solution.py:181
  193.0 4.1 all-to-all-start.1
  197.8 5.0 all-gather.6.cloned.1.call-done
  202.8 5.0 slice.285
  207.8 5.8 slice.288
  213.5 1.3 fusion.16
  214.9 2.1 convert_bitcast_fusion.1
  217.0 2.6 copy.168
  219.5 2.8 fusion.72
  222.3 4.0 multiply_reduce_fusion.15
  226.3 69.7 %all-gather.8.cloned.1.call-done = bf16[1024,5632]{1,0:T(8,128)(2,1)} async-done(((bf16[32,5632]{1,0:T(8,128)(2,1)}), bf16[1024,5632]{1,0:T(8,128)(2,1)}) %all-gather.8.cloned.1.call-update) | async-done | bytes 11534352 | tf_op jit(solution)/shard_map/all_gather | solution.py:305
  296.0 6.3 fusion.66
  302.4 6.1 fusion.2
  308.5 6.3 multiply_reduce_fusion.13
  314.8 1.3 fusion.26
  316.1 1.2 convolution_convert_fusion.3
  317.4 1.7 convolution_convert_fusion.2
  319.1 7.7 pad_maximum_fusion
  326.8 9.0 %convolution_convert_fusion.1 = bf16[1024,5632]{1,0:T(8,128)(2,1)} fusion(bf16[128,2816]{1,0:T(8,128)(2,1)} %get-tuple-element.201, bf16[128,2816]{1,0:T(8,128)(2,1)} %copy-done.35, f32[128,1024]{1,0:T(8,128)} %get-tuple-element.255, f32[1024]{0:T(1024)S(1)} %copy-done.42, f32[128]{0:T(128)S(1)} %fusion.62), kind=kOutput, calls=%fused_computation.1 | convolution fusion | flops 1485438976 | bytes 13505024 | tf_op jit(solution)/shard_map/dot_general | solution.py:16
  335.8 2.6 copy.174
  338.4 5.6 fusion.15
  344.0 2.2 fusion.6
  346.2 4.3 all-to-all-start.2
  350.5 12.1 %all-to-all-done.2 = bf16[4,1,2,128,256]{4,3,2,1,0:T(8,128)(2,1)} async-done(((bf16[4,1,2,128,256]{4,3,2,1,0:T(8,128)(2,1)}), bf16[4,1,2,128,256]{4,3,2,1,0:T(8,128)(2,1)}, u32[]{:S(2)}, u32[]{:S(2)}) %all-to-all-start.2) | async-done | bytes 524320 | tf_op jit(solution)/shard_map/all_to_all | solution.py:265
  362.6 1.2 convert_bitcast_fusion.2
  364.2 27.4 %recurrence_backward.1 = (f32[2,512,128]{2,1,0:T(8,128)S(1)}, f32[2,512,128]{2,1,0:T(8,128)S(1)}, f32[2,512,256]{2,1,0:T(8,128)S(1)}, f32[2,512,128]{2,1,0:T(8,128)S(1)}, f32[2,512,128]{2,1,0:T(8,128)S(1)}) custom-call(f32[2,512,128]{2,1,0:T(8,128)S(1)} %multiply_bitcast_fusion.2.q_ref, f32[2,512,128]{2,1,0:T(8,128)S(1)} %multiply_bitcast_fusion.1.k_ref, ...), custom_call_target="tpu_custom_call" | custom-call | flops 960000000 | bytes 12000000 | tf_op jit(solution)/shard_map/recurrence_backward/pallas_call | solution.py:211
  395.8 1.4 reduce_sum.273
  397.2 1.0 copy.179
  398.3 1.3 reduce_sum.268
  400.6 1.4 fusion.45
  402.3 2.2 multiply_reduce_fusion.8
  410.9 1.2 copy.212
  412.1 3.5 all-to-all-start.3
  416.2 23.1 %all-to-all-done.3 = bf16[4,1,2,128,640]{4,3,2,1,0:T(8,128)(2,1)S(1)} async-done(((bf16[4,1,2,128,640]{4,3,2,1,0:T(8,128)(2,1)}), bf16[4,1,2,128,640]{4,3,2,1,0:T(8,128)(2,1)S(1)}, u32[]{:S(2)}, u32[]{:S(2)}) %all-to-all-start.3) | async-done | bytes 1310752 | tf_op jit(solution)/shard_map/all_to_all | solution.py:274
  440.4 1.1 copy.183
  441.5 1.0 copy.184
  444.4 1.4 slice_reduce_fusion
  445.8 1.1 constant_dynamic-update-slice_fusion.3
  447.0 6.7 convolution_convert_fusion
  454.3 9.9 %fusion.25 = (f32[1024]{0:T(1024)S(1)}, f32[128]{0:T(128)S(1)}, f32[128,1024]{1,0:T(8,128)}) fusion(bf16[1,128,1024]{2,1,0:T(8,128)(2,1)S(1)} %copy-done.16, f32[128]{0:T(128)S(1)} %fusion.61, f32[1024]{0:T(1024)S(1)} %copy-done.43, bf16[128,6160]{0,1:T(8,128)(2,1)S(1)} %constant_dynamic-update-slice_fusion, bf16[1024,6160]{1,0:T(8,128)(2,1)} %all-gather.4.cloned.1.call-done), kind=kOutput, calls=%fused_computation.82 | convolution fusion | flops 1615723392 | bytes 14988288 | tf_op jit(solution)/shard_map/dot_general | solution.py:16
  464.4 1.3 collective-permute-done
  465.7 4.8 collective-permute-done.1
  470.6 2.3 collective-permute-start.2
  472.9 4.3 fusion.5
  477.6 3.4 collective-permute-start.3
  481.0 2.4 collective-permute-done.3
  485.1 2.8 collective-permute-done.4
  491.5 1.6 slice.307
  493.1 1.7 slice.311
  494.8 150.3 %reduce-scatter.8.cloned.1.call-done = bf16[32,5632]{1,0:T(8,128)(2,1)} async-done(((bf16[1024,5632]{1,0:T(8,128)(2,1)}), bf16[32,5632]{1,0:T(8,128)(2,1)}) %reduce-scatter.8.cloned.1.call-update) | async-done | bytes 360464 | tf_op jit(solution)/shard_map/reduce_scatter | solution.py:309
  645.1 1.9 fusion.79
  647.0 163.1 %reduce-scatter.4.cloned.1.call-done = bf16[32,6160]{1,0:T(8,128)(2,1)} async-done(((bf16[1024,6160]{1,0:T(8,128)(2,1)}), bf16[32,6160]{1,0:T(8,128)(2,1)}) %reduce-scatter.4.cloned.1.call-update) | async-done | bytes 394256 | tf_op jit(solution)/shard_map/reduce_scatter | solution.py:309
  812.3 1.6 fusion.78
  813.9 1.8 fusion.77
  (221 shorter events, 36.4 us)
Async XLA Ops:
  7.2 7.2 copy-start.16
  7.2 104.4 %copy-start.43 = (f32[1024]{0:T(1024)S(1)}, f32[1024]{0:T(1024)}, u32[]{:S(2)}) copy-start(f32[1024]{0:T(1024)} %param.21) | copy-start | bytes 12292
  7.2 104.4 %all-gather.4.cloned.1.call-start = ((), (), s32[]{:S(2)}) async-start(), calls=%async_computation.7 | async-start | bytes 13246464 | tf_op jit(solution)/shard_map/all_gather | solution.py:305
  10.7 192.1 %all-gather.6.cloned.1.call-start = ((), (), s32[]{:S(2)}) async-start(), calls=%async_computation.8 | async-start | bytes 10272768 | tf_op jit(solution)/shard_map/all_gather | solution.py:305
  12.5 283.5 %all-gather.8.cloned.1.call-start = ((), (), s32[]{:S(2)}) async-start(), calls=%async_computation.9 | async-start | bytes 11894784 | tf_op jit(solution)/shard_map/all_gather | solution.py:305
  125.6 6.1 copy-start.45
  125.6 6.2 copy-start.46
  126.9 26.8 %all-to-all-start = ((bf16[4,1,2,128,640]{4,3,2,1,0:T(8,128)(2,1)}), bf16[4,1,2,128,640]{4,3,2,1,0:T(8,128)(2,1)S(1)}, u32[]{:S(2)}, u32[]{:S(2)}) async-start(bf16[4,1,2,128,640]{4,3,2,1,0:T(8,128)(2,1)} %maximum_bitcast_fusion), calls=%async_computation | async-start | bytes 2621440 | tf_op jit(solution)/shard_map/all_to_all | solution.py:265
  154.0 1.7 copy-start.12
  154.1 2.7 copy-start.17
  154.2 2.4 copy-start.30
  154.2 2.6 copy-start.32
  155.0 1.6 copy-start.21
  155.0 1.6 copy-start.19
  191.0 1.0 copy-start.6
  191.1 1.1 copy-start.10
  191.1 6.7 copy-start.44
  193.0 20.5 %all-to-all-start.1 = ((bf16[4,1,2,128,256]{4,3,2,1,0:T(8,128)(2,1)}), bf16[4,1,2,128,256]{4,3,2,1,0:T(8,128)(2,1)}, u32[]{:S(2)}, u32[]{:S(2)}) async-start(bf16[4,1,2,128,256]{4,3,2,1,0:T(8,128)(2,1)} %bitcast.242), calls=%async_computation.1 | async-start | bytes 1048576 | tf_op jit(solution)/shard_map/all_to_all | solution.py:274
  197.2 294.4 %reduce-scatter.6.cloned.1.call-start = ((), (), s32[]{:S(2)}) async-start(), calls=%async_computation.11 | async-start | bytes 10272768 | tf_op jit(solution)/shard_map/reduce_scatter | solution.py:309
  222.3 4.0 copy-start.23
  222.3 73.7 %copy-start.42 = (f32[1024]{0:T(1024)S(1)}, f32[1024]{0:T(1024)}, u32[]{:S(2)}) copy-start(f32[1024]{0:T(1024)} %param.35) | copy-start | bytes 12292
  296.0 6.3 copy-start.39
  296.0 12.4 %slice-start = ((s8[11534336]{0:T(1024)(128)(4,1)}), s8[4194304]{0:T(1024)(128)(4,1)S(1)}, s32[]{:S(2)}) async-start(s8[11534336]{0:T(1024)(128)(4,1)} %bitcast.217), calls=%async_computation.13 | async-start | bytes 8388608
  296.0 12.4 %slice-start.1 = ((s8[11534336]{0:T(1024)(128)(4,1)}), s8[4194304]{0:T(1024)(128)(4,1)S(1)}, s32[]{:S(2)}) async-start(s8[11534336]{0:T(1024)(128)(4,1)} %bitcast.217), calls=%async_computation.14 | async-start | bytes 8388608
  302.4 6.1 slice-start.2
  302.4 6.1 copy-start.14
  308.4 6.3 copy-start.35
  308.4 8.9 %copy-start.26 = (bf16[128,2816]{1,0:T(8,128)(2,1)}, bf16[128,2816]{1,0:T(8,128)(2,1)S(1)}, u32[]{:S(2)}) copy-start(bf16[128,2816]{1,0:T(8,128)(2,1)S(1)} %get-tuple-element.205) | copy-start | bytes 2162692
  308.5 7.6 copy-start.24
  316.1 1.3 copy-start.28
  316.1 1.3 copy-start.40
  326.8 318.3 %reduce-scatter.8.cloned.1.call-start = ((), (), s32[]{:S(2)}) async-start(), calls=%async_computation.12 | async-start | bytes 11894784 | tf_op jit(solution)/shard_map/reduce_scatter | solution.py:309
  346.2 16.4 %all-to-all-start.2 = ((bf16[4,1,2,128,256]{4,3,2,1,0:T(8,128)(2,1)}), bf16[4,1,2,128,256]{4,3,2,1,0:T(8,128)(2,1)}, u32[]{:S(2)}, u32[]{:S(2)}) async-start(bf16[4,1,2,128,256]{4,3,2,1,0:T(8,128)(2,1)} %bitcast.244), calls=%async_computation.2 | async-start | bytes 1048576 | tf_op jit(solution)/shard_map/all_to_all | solution.py:265
  362.6 1.4 copy-start.7
  362.6 1.5 copy-start.11
  391.6 0.8 copy-start
  393.2 1.0 copy-start.4
  394.2 0.8 copy-start.8
  395.0 0.8 copy-start.9
  395.8 6.2 copy-start.22
  395.8 6.5 copy-start.20
  395.8 6.5 copy-start.31
  395.8 6.6 copy-start.33
  395.8 6.2 copy-start.1
  395.8 6.6 copy-start.3
  404.7 1.2 copy-start.34
  404.9 1.4 copy-start.5
  404.9 2.3 copy-start.13
  404.9 2.5 copy-start.18
  408.6 1.0 copy-start.37
  408.6 1.2 copy-start.38
  410.9 5.1 copy-start.41
  412.1 27.3 %all-to-all-start.3 = ((bf16[4,1,2,128,640]{4,3,2,1,0:T(8,128)(2,1)}), bf16[4,1,2,128,640]{4,3,2,1,0:T(8,128)(2,1)S(1)}, u32[]{:S(2)}, u32[]{:S(2)}) async-start(bf16[4,1,2,128,640]{4,3,2,1,0:T(8,128)(2,1)} %bitcast.212), calls=%async_computation.3 | async-start | bytes 2621440 | tf_op jit(solution)/shard_map/all_to_all | solution.py:274
  415.6 394.5 %reduce-scatter.4.cloned.1.call-start = ((), (), s32[]{:S(2)}) async-start(), calls=%async_computation.10 | async-start | bytes 13246464 | tf_op jit(solution)/shard_map/reduce_scatter | solution.py:309
  439.3 4.1 copy-start.25
  454.3 18.6 %copy-start.15 = (f32[128,1024]{1,0:T(8,128)S(1)}, f32[128,1024]{1,0:T(8,128)}, u32[]{:S(2)}) copy-start(f32[128,1024]{1,0:T(8,128)} %get-tuple-element.255) | copy-start | bytes 1572868
  454.3 18.6 %copy-start.27 = (bf16[128,2816]{1,0:T(8,128)(2,1)S(1)}, bf16[128,2816]{1,0:T(8,128)(2,1)}, u32[]{:S(2)}) copy-start(bf16[128,2816]{1,0:T(8,128)(2,1)} %copy-done.26) | copy-start | bytes 2162692
  464.3 1.3 collective-permute-start
  465.7 4.9 collective-permute-start.1
  470.6 13.5 %copy-start.29 = (f32[128,1024]{1,0:T(8,128)S(1)}, f32[128,1024]{1,0:T(8,128)}, u32[]{:S(2)}) copy-start(f32[128,1024]{1,0:T(8,128)} %copy-done.28) | copy-start | bytes 1572868
  470.6 13.5 %copy-start.36 = (f32[128,1024]{1,0:T(8,128)S(1)}, f32[128,1024]{1,0:T(8,128)}, u32[]{:S(2)}) copy-start(f32[128,1024]{1,0:T(8,128)} %get-tuple-element.257) | copy-start | bytes 1572868
  470.6 7.0 collective-permute-start.2
  477.6 5.8 collective-permute-start.3
  483.4 4.5 collective-permute-start.4
  (1 other events, 0.8 us)
Sparse Core Ops, SparseCore 0:
  11.5 100.0 all-gather.3
  115.0 87.7 all-gather.5
  206.2 89.7 all-gather.7
  326.9 156.5 reduce-scatter.5
  485.7 159.3 reduce-scatter.7
  647.4 162.6 reduce-scatter.3

commit v2 on v1

--- a/solution.py
+++ b/solution.py
@@ -305,10 +305,57 @@
     return lax.all_gather(shard, ("seq", "fsdp"), axis=0, tiled=True)
 
 
-def scatter(partial):
-    return lax.psum_scatter(
-        partial.astype(jnp.bfloat16), ("seq", "fsdp"), scatter_dimension=0, tiled=True
-    ).astype(jnp.float32)
+def mesh_bits():
+    seq, fsdp = lax.axis_size("seq"), lax.axis_size("fsdp")
+    seq_bits = [("seq", 1 << b) for b in range(seq.bit_length() - 1)]
+    fsdp_bits = [("fsdp", 1 << b) for b in range(fsdp.bit_length() - 1)]
+    return seq_bits, fsdp_bits
+
+
+def halving_order(kind):
+    seq_bits, fsdp_bits = mesh_bits()
+    far = fsdp_bits[1:]
+    if kind == 0:
+        return seq_bits + far
+    if kind == 1:
+        return seq_bits[1:] + far + seq_bits[:1]
+    return far[:1] + seq_bits + far[1:]
+
+
+def swap(part, axis, bit):
+    return lax.ppermute(part, axis, [(i, i ^ bit) for i in range(lax.axis_size(axis))])
+
+
+def summed_term(left, right, kind):
+    seq, fsdp = lax.axis_size("seq"), lax.axis_size("fsdp")
+    count = seq * fsdp
+    if seq & (seq - 1) or fsdp & (fsdp - 1) or fsdp < 2:
+        return lax.psum_scatter(
+            column_term(left, right), ("seq", "fsdp"), scatter_dimension=0, tiled=True
+        )
+    rows = left.shape[1] // count
+    columns = right.shape[1]
+    paired = left.reshape(left.shape[0], count // 2, 2, rows)
+    core = lax.axis_index("fsdp") % 2
+
+    def half(which):
+        chosen = lax.dynamic_index_in_dim(paired, which, 2, keepdims=False)
+        return column_term(chosen.reshape(left.shape[0], count // 2 * rows), right)
+
+    arrived = swap(half(1 - core).astype(jnp.bfloat16), "fsdp", 1)
+    total = half(core) + arrived.astype(jnp.float32)
+    seq_bits, fsdp_bits = mesh_bits()
+    live = seq_bits[::-1] + fsdp_bits[:0:-1]
+    for axis, bit in halving_order(kind):
+        place = live.index((axis, bit))
+        before, after = 1 << place, 1 << (len(live) - 1 - place)
+        split = total.astype(jnp.bfloat16).reshape(before, 2, after * rows, columns)
+        mine = (lax.axis_index(axis) // bit) % 2
+        keep = lax.dynamic_index_in_dim(split, mine, 1, keepdims=False)
+        send = lax.dynamic_index_in_dim(split, 1 - mine, 1, keepdims=False)
+        total = keep.astype(jnp.float32) + swap(send, axis, bit).astype(jnp.float32)
+        live.remove((axis, bit))
+    return total.reshape(rows, columns)
 
 
 def out_piece(values, gate_values, gain):
@@ -452,20 +499,12 @@
     grad_mixed = to_heads(
         grad_returned.astype(jnp.bfloat16).reshape(batches, positions, head_count, head_v)
     )
-    ffn_sum = scatter(column_term(normed2_b, ffn_grads))
-    tall_sum = scatter(
-        jnp.concatenate(
-            [
-                column_term(normed_out_b, grad_hidden_b).astype(jnp.bfloat16).reshape(
-                    count, out_rows, width
-                ),
-                column_term(mid_b, grad_out_b).astype(jnp.bfloat16).reshape(
-                    count, down_rows, width
-                ),
-            ],
-            axis=1,
-        ).reshape(count * (out_rows + down_rows), width)
-    )
+    down_sum = summed_term(mid_b, grad_out_b, 0)
+    sum_wm = summed_term(normed2_b, ffn_grads[:, :ff_width], 1)
+    sum_wu = summed_term(normed2_b, ffn_grads[:, ff_width:], 2)
+    out_sum = summed_term(normed_out_b, grad_hidden_b, 0)
+    grad_gate_b = grad_gate_heads.reshape(row_count, value_dim).astype(jnp.bfloat16)
+    sum_wg = summed_term(normed_b, grad_gate_b, 1)
     prepared_grads = run_backward(
         *prepared,
         memories,
@@ -477,7 +516,6 @@
     )
     back = to_positions(grad_moved.astype(jnp.bfloat16)).reshape(row_count, head_count, -1)
     edge = 2 * head_k + head_v
-    grad_gate_b = grad_gate_heads.reshape(row_count, value_dim).astype(jnp.bfloat16)
     mixer_grads = jnp.concatenate(
         [
             back[:, :, :head_k].reshape(row_count, key_dim),
@@ -489,7 +527,20 @@
         ],
         axis=1,
     )
-    mixer_sum = scatter(column_term(normed_b, mixer_grads))
+    third = edge_three // 384 * 128
+    logit_grads = jnp.concatenate([back[:, :, edge], back[:, :, edge + 1]], axis=1)
+    qkv_sum = jnp.concatenate(
+        [
+            summed_term(normed_b, mixer_grads[:, :third], 0),
+            summed_term(normed_b, mixer_grads[:, third : 2 * third], 1),
+            summed_term(
+                normed_b,
+                jnp.concatenate([mixer_grads[:, 2 * third : edge_three], logit_grads], axis=1),
+                2,
+            ),
+        ],
+        axis=1,
+    )
     normed_gradient = bf_dot(mixer_grads, mixer_w.T)
     grad_flat, grad_attn_gain = pull_first(normed_gradient)
     grad_tokens = (grad_flat + grad_hidden).reshape(tokens.shape)
@@ -514,23 +565,23 @@
         result,
         grad_tokens,
         sum_attn,
-        mixer_sum[:, :key_dim],
-        mixer_sum[:, key_dim:edge_two],
-        mixer_sum[:, edge_two:edge_three],
-        mixer_sum[:, edge_three:edge_four],
-        mixer_sum[:, edge_four:edge_five],
-        mixer_sum[:, edge_five:],
+        qkv_sum[:, :key_dim],
+        qkv_sum[:, key_dim:edge_two],
+        qkv_sum[:, edge_two:edge_three],
+        sum_wg,
+        qkv_sum[:, edge_three : edge_three + head_count],
+        qkv_sum[:, edge_three + head_count :],
         sum_cq,
         sum_ck,
         sum_cv,
         sum_rate,
         sum_bias,
         sum_out_gain,
-        tall_sum[:out_rows],
+        out_sum,
         sum_mlp_gain,
-        ffn_sum[:, :ff_width],
-        ffn_sum[:, ff_width:],
-        tall_sum[out_rows:],
+        sum_wm,
+        sum_wu,
+        down_sum,
     )
 
 

time: 831 us -> 702 us (0.84)
  waiting for transfers between devices: 552 us -> 349 us
  starting transfers between devices: 23.3 us -> 54 us
  matrix products: 72.5 us -> 88.4 us
  other arithmetic: 38.2 us -> 54.1 us
  local copies, waits for them, and re-layouts: 61.6 us -> 72.7 us
    reduce_scatter x3 -> x0, waiting for transfers between devices: 313 us -> none  [scatter(): lax.psum_scatter(partial.astype(jnp.bfloat16), ('seq', 'fsdp'), scatter_d...]
    ppermute x0 -> x40, waiting for transfers between devices: none -> 144 us  [swap(): lax.ppermute(part, axis, [(i, i ^ bit) for i in range(lax.axis_size(axis))])]
    ppermute x0 -> x40, starting transfers between devices: none -> 31.5 us  [swap(): lax.ppermute(part, axis, [(i, i ^ bit) for i in range(lax.axis_size(axis))])]
    convert_element_type x0 -> x26, other arithmetic: none -> 16.3 us  [the longest x24 14.3 us: summed_term(): split = total.astype(jnp.bfloat16).reshape(before, 2, after * rows, columns)]
    dot_general x12 -> x24, matrix products: 72.5 us -> 88.4 us  [bf_dot(): return jnp.dot(left, right, preferred_element_type=jnp.float32)]
    squeeze x0 -> x32, local copies, waits for them, and re-layouts: none -> 13 us  [summed_term(): send = lax.dynamic_index_in_dim(split, 1 - mine, 1, keepdims=False)]
    all_to_all x2, waiting for transfers between devices: 32 us -> 19.8 us  [to_heads(): lax.all_to_all(split, 'seq', split_axis=0, concat_axis=0, tiled=True)]
    all_gather x3, waiting for transfers between devices: 172 us -> 160 us  [gather(): return lax.all_gather(shard, ('seq', 'fsdp'), axis=0, tiled=True)]
  transfers between devices with their start and end apart: 15 -> 52, of which waited for: 13 -> 28; matrix products, arithmetic and copies ran while one was open for 15% -> 24% of each run, Pallas kernels for 7% -> 9%
where the time goes in v2:
time: 702 us; the launch traced here: 694 us
  waiting for transfers between devices  349 us (50%)
  matrix products  88.4 us (13%)
  local copies, waits for them, and re-layouts  72.7 us (10%)
  Pallas kernels  59.6 us (8%)
  other arithmetic  54.1 us (8%)
  starting transfers between devices  54 us (8%)
  between operations  16.4 us (2%)
    all_gather x3, waiting for transfers between devices, gather(): return lax.all_gather(shard, ('seq', 'fsdp'), axis=0, tiled=True)  160 us
    ppermute x40, waiting for transfers between devices, swap(): lax.ppermute(part, axis, [(i, i ^ bit) for i in range(lax.axis_size(axis))])  144 us
    dot_general x24, matrix products, bf_dot(): return jnp.dot(left, right, preferred_element_type=jnp.float32)  88.4 us
    pallas_call x1, Pallas kernels, run_forward(): pl.pallas_call(forward_kernel, grid=(chunks,), in_specs=[narrow, narrow,...  32.2 us
    ppermute x40, starting transfers between devices, swap(): lax.ppermute(part, axis, [(i, i ^ bit) for i in range(lax.axis_size(axis))])  31.5 us
    pallas_call x1, Pallas kernels, run_backward(): pl.pallas_call(backward_kernel, grid=(chunks,), in_specs=[narrow, narrow,...  27.4 us
    all_to_all x2, waiting for transfers between devices, to_heads(): lax.all_to_all(split, 'seq', split_axis=0, concat_axis=0, tiled=True)  19.8 us
    all_to_all x2, waiting for transfers between devices, to_positions(): lax.all_to_all(split, 'seq', split_axis=0, concat_axis=0, tiled=True)  16 us
  transfers between devices with their start and end apart: 52, of which 28 were waited for; matrix products, arithmetic and copies ran while one was open for 24% of the time, Pallas kernels for 9%

profile of v2, /device:TPU:0, one launch (start us, length us, event | category | flops | bytes accessed | tf_op | source)
XLA Modules:
  0.0 694.1 jit_solution(15845414164014936299)
XLA Ops:
  13.6 98.0 %all-gather.4.cloned.1.call-done = bf16[1024,6160]{1,0:T(8,128)(2,1)} async-done(((bf16[32,6160]{1,0:T(8,128)(2,1)}), bf16[1024,6160]{1,0:T(8,128)(2,1)}) %all-gather.4.cloned.1.call-update) | async-done | bytes 12615696 | tf_op jit(solution)/shard_map/all_gather | solution.py:305
  111.6 11.4 %fusion.118 = (bf16[128,6160]{0,1:T(8,128)(2,1)S(1)}, f32[128,6160]{0,1:T(8,128)}) fusion(bf16[1024,6160]{1,0:T(8,128)(2,1)} %all-gather.4.cloned.1.call-done, bf16[1,128,1024]{2,1,0:T(8,128)(2,1)S(1)} %copy-done.21, f32[1024]{0:T(1024)S(1)} %copy-done.69, f32[128]{0:T(128)S(1)} %fusion.91), kind=kOutput, calls=%fused_computation.348 | convolution fusion | flops 1616119808 | bytes 17613312 | tf_op jit(solution)/shard_map/dot_general | solution.py:16
  126.9 3.7 all-to-all-start
  133.7 19.8 %all-to-all-done = bf16[4,1,2,128,640]{4,3,2,1,0:T(8,128)(2,1)S(1)} async-done(((bf16[4,1,2,128,640]{4,3,2,1,0:T(8,128)(2,1)}), bf16[4,1,2,128,640]{4,3,2,1,0:T(8,128)(2,1)S(1)}, u32[]{:S(2)}, u32[]{:S(2)}) %all-to-all-start) | async-done | bytes 1310752 | tf_op jit(solution)/shard_map/all_to_all | solution.py:265
  158.5 32.2 %recurrence_forward.1 = (f32[2,512,256]{2,1,0:T(8,128)S(1)}, f32[4,2,128,256]{3,2,1,0:T(8,128)S(1)}, f32[4,2,128,128]{3,2,1,0:T(8,128)S(1)}) custom-call(f32[2,512,128]{2,1,0:T(8,128)S(1)} %multiply_bitcast_fusion.2.q_ref, f32[2,512,128]{2,1,0:T(8,128)S(1)} %multiply_bitcast_fusion.1.k_ref, f32[2,512,256]{2,1,0:T(8,128)S(1)} %get-tuple-element.194.v_ref, ...), custom_call_target="tpu_custom_call" | custom-call | flops 480000000 | bytes 8000000 | tf_op jit(solution)/shard_map/recurrence_forward/pallas_call | solution.py:181
  192.8 4.4 all-to-all-start.1
  200.8 2.3 all-gather.6.cloned.1.call-done
  203.1 4.8 slice.283
  207.9 5.8 slice.286
  215.6 2.1 convert_bitcast_fusion.1
  217.7 2.5 copy.206
  220.3 3.0 fusion.111
  223.3 2.6 copy.212
  225.9 3.2 multiply_reduce_fusion.15
  236.2 59.8 %all-gather.8.cloned.1.call-done = bf16[1024,5632]{1,0:T(8,128)(2,1)} async-done(((bf16[32,5632]{1,0:T(8,128)(2,1)}), bf16[1024,5632]{1,0:T(8,128)(2,1)}) %all-gather.8.cloned.1.call-update) | async-done | bytes 11534352 | tf_op jit(solution)/shard_map/all_gather | solution.py:305
  296.0 6.1 fusion.119
  302.1 6.3 fusion.8
  308.4 2.2 copy.233
  310.6 2.0 constant_dynamic-slice_fusion.4
  312.7 3.7 convolution_convert_fusion.1
  316.4 2.5 convolution_convert_fusion
  318.9 8.9 %multiply_reduce_fusion.13 = (f32[1024]{0:T(1024)}, f32[128]{0:T(128)S(1)}, f32[128,1024]{1,0:T(8,128)S(1)}) fusion(f32[128,1024]{1,0:T(8,128)S(1)} %copy-done.15, f32[128]{0:T(128)S(1)} %copy-done.106, f32[1024]{0:T(1024)S(1)} %copy-done.70, bf16[1024,5632]{1,0:T(8,128)(2,1)} %all-gather.8.cloned.1.call-done, bf16[128,2816]{1,0:T(8,128)(2,1)S(1)} %copy-done.36, ...), kind=kOutput, calls=%fused_computation.187 | convolution fusion | flops 1480063872 | bytes 14033920 | tf_op jit(solution)/shard_map/dot_general | solution.py:16
  328.1 5.1 fusion.30
  333.2 2.2 fusion.20
  335.4 4.1 all-to-all-start.2
  339.6 2.1 copy.224
  341.6 3.2 convolution_convert_fusion.7
  344.9 2.0 convolution_convert_fusion.3
  347.4 2.5 convolution_convert_fusion.2
  350.4 4.3 fusion.19
  356.2 27.4 %recurrence_backward.1 = (f32[2,512,128]{2,1,0:T(8,128)S(1)}, f32[2,512,128]{2,1,0:T(8,128)S(1)}, f32[2,512,256]{2,1,0:T(8,128)S(1)}, f32[2,512,128]{2,1,0:T(8,128)S(1)}, f32[2,512,128]{2,1,0:T(8,128)S(1)}) custom-call(f32[2,512,128]{2,1,0:T(8,128)S(1)} %multiply_bitcast_fusion.2.q_ref, f32[2,512,128]{2,1,0:T(8,128)S(1)} %multiply_bitcast_fusion.1.k_ref, ...), custom_call_target="tpu_custom_call" | custom-call | flops 960000000 | bytes 12000000 | tf_op jit(solution)/shard_map/recurrence_backward/pallas_call | solution.py:211
  383.7 3.8 multiply_reduce_fusion.2
  390.9 4.2 multiply_reduce_fusion.8
  397.0 2.0 fusion.106
  401.3 4.1 all-to-all-start.3
  406.0 16.0 %all-to-all-done.3 = bf16[4,1,2,128,640]{4,3,2,1,0:T(8,128)(2,1)S(1)} async-done(((bf16[4,1,2,128,640]{4,3,2,1,0:T(8,128)(2,1)}), bf16[4,1,2,128,640]{4,3,2,1,0:T(8,128)(2,1)S(1)}, u32[]{:S(2)}, u32[]{:S(2)}) %all-to-all-start.3) | async-done | bytes 1310752 | tf_op jit(solution)/shard_map/all_to_all | solution.py:274
  423.7 9.1 %fusion.63 = (f32[1024]{0:T(1024)S(1)}, f32[128]{0:T(128)S(1)}, f32[128,1024]{1,0:T(8,128)S(1)}) fusion(bf16[1,128,1024]{2,1,0:T(8,128)(2,1)S(1)} %copy-done.21, f32[128]{0:T(128)S(1)} %copy-done.104, f32[1024]{0:T(1024)S(1)} %copy-done.69, bf16[128,6160]{0,1:T(8,128)(2,1)S(1)} %constant_dynamic-update-slice_fusion.3, ...), kind=kOutput, calls=%fused_computation.172 | convolution fusion | flops 1615723392 | bytes 14988288 | tf_op jit(solution)/shard_map/dot_general | solution.py:16
  436.4 2.3 collective-permute-done.1
  442.3 2.6 collective-permute-done.2
  458.1 2.4 add_convert_fusion.3
  462.3 2.3 add_convert_fusion.4
  473.6 2.7 add_convert_fusion.2
  479.0 2.8 add_convert_fusion
  488.2 3.5 copy.229
  493.0 6.4 collective-permute-done.26
  499.9 1.9 fusion.3
  505.1 8.3 %collective-permute-done.6 = bf16[2,128,1280]{2,1,0:T(8,128)(2,1)} collective-permute-done((bf16[2,128,1280]{2,1,0:T(8,128)(2,1)}, bf16[2,128,1280]{2,1,0:T(8,128)(2,1)}, u32[]{:S(2)}, u32[]{:S(2)}) %collective-permute-start.6) | collective-permute-done | bytes 655392 | tf_op jit(solution)/shard_map/ppermute | solution.py:326
  517.0 30.7 %collective-permute-done.7 = bf16[1,128,1280]{2,1,0:T(8,128)(2,1)S(1)} collective-permute-done((bf16[1,128,1280]{2,1,0:T(8,128)(2,1)S(1)}, bf16[1,128,1280]{2,1,0:T(8,128)(2,1)S(1)}, u32[]{:S(2)}, u32[]{:S(2)}) %collective-permute-start.7) | collective-permute-done | bytes 327712 | tf_op jit(solution)/shard_map/ppermute | solution.py:326
  548.2 8.9 %collective-permute-done.12 = bf16[4,32,1280]{2,1,0:T(8,128)(2,1)S(1)} collective-permute-done((bf16[4,32,1280]{2,1,0:T(8,128)(2,1)S(1)}, bf16[4,32,1280]{2,1,0:T(8,128)(2,1)S(1)}, u32[]{:S(2)}, u32[]{:S(2)}) %collective-permute-start.12) | collective-permute-done | bytes 327712 | tf_op jit(solution)/shard_map/ppermute | solution.py:326
  558.7 11.0 %collective-permute-done.27 = bf16[1,256,1024]{2,1,0:T(8,128)(2,1)S(1)} collective-permute-done((bf16[1,256,1024]{2,1,0:T(8,128)(2,1)S(1)}, bf16[1,256,1024]{2,1,0:T(8,128)(2,1)S(1)}, u32[]{:S(2)}, u32[]{:S(2)}) %collective-permute-start.27) | collective-permute-done | bytes 524320 | tf_op jit(solution)/shard_map/ppermute | solution.py:326
  571.7 20.3 %collective-permute-done.16 = bf16[8,32,1552]{2,1,0:T(8,128)(2,1)S(1)} collective-permute-done((bf16[8,32,1552]{2,1,0:T(8,128)(2,1)S(1)}, bf16[8,32,1552]{2,1,0:T(8,128)(2,1)S(1)}, u32[]{:S(2)}, u32[]{:S(2)}) %collective-permute-start.16) | collective-permute-done | bytes 794656 | tf_op jit(solution)/shard_map/ppermute | solution.py:326
  593.9 4.6 collective-permute-done.8
  600.1 3.0 collective-permute-done.14
  603.0 6.2 collective-permute-done.9
  610.0 5.6 collective-permute-done.28
  617.3 6.6 collective-permute-done.29
  625.3 3.7 collective-permute-done.24
  637.0 1.9 collective-permute-start.19
  640.4 9.2 %collective-permute-done.19 = bf16[1,32,1552]{2,1,0:T(8,128)(2,1)S(1)} collective-permute-done((bf16[1,32,1552]{2,1,0:T(8,128)(2,1)S(1)}, bf16[1,32,1552]{2,1,0:T(8,128)(2,1)S(1)}, u32[]{:S(2)}, u32[]{:S(2)}) %collective-permute-start.19) | collective-permute-done | bytes 99360 | tf_op jit(solution)/shard_map/ppermute | solution.py:326
  655.1 3.4 collective-permute-start.33
  660.9 3.4 collective-permute-start.39
  664.3 13.3 %collective-permute-done.33 = bf16[2,32,2816]{2,1,0:T(8,128)(2,1)S(1)} collective-permute-done((bf16[2,32,2816]{2,1,0:T(8,128)(2,1)S(1)}, bf16[2,32,2816]{2,1,0:T(8,128)(2,1)S(1)}, u32[]{:S(2)}, u32[]{:S(2)}) %collective-permute-start.33) | collective-permute-done | bytes 360480 | tf_op jit(solution)/shard_map/ppermute | solution.py:326
  681.2 2.1 collective-permute-done.34
  684.1 2.5 collective-permute-done.44
  (531 shorter events, 126.6 us)
Async XLA Ops:
  7.2 104.4 %copy-start.69 = (f32[1024]{0:T(1024)S(1)}, f32[1024]{0:T(1024)}, u32[]{:S(2)}) copy-start(f32[1024]{0:T(1024)} %param.21) | copy-start | bytes 12292
  7.2 104.4 %all-gather.4.cloned.1.call-start = ((), (), s32[]{:S(2)}) async-start(), calls=%async_computation.4 | async-start | bytes 13246464 | tf_op jit(solution)/shard_map/all_gather | solution.py:305
  10.8 192.3 %all-gather.6.cloned.1.call-start = ((), (), s32[]{:S(2)}) async-start(), calls=%async_computation.5 | async-start | bytes 10272768 | tf_op jit(solution)/shard_map/all_gather | solution.py:305
  12.6 283.4 %all-gather.8.cloned.1.call-start = ((), (), s32[]{:S(2)}) async-start(), calls=%async_computation.6 | async-start | bytes 11894784 | tf_op jit(solution)/shard_map/all_gather | solution.py:305
  13.6 109.4 %copy-start.122 = (f32[128]{0:T(128)}, f32[128]{0:T(128)S(1)}, u32[]{:S(2)}) copy-start(f32[128]{0:T(128)S(1)} %fusion.64) | copy-start | bytes 1540
  13.6 185.2 %copy-start.103 = (f32[128]{0:T(128)}, f32[128]{0:T(128)S(1)}, u32[]{:S(2)}) copy-start(f32[128]{0:T(128)S(1)} %fusion.91) | copy-start | bytes 1540
  126.9 26.6 %all-to-all-start = ((bf16[4,1,2,128,640]{4,3,2,1,0:T(8,128)(2,1)}), bf16[4,1,2,128,640]{4,3,2,1,0:T(8,128)(2,1)S(1)}, u32[]{:S(2)}, u32[]{:S(2)}) async-start(bf16[4,1,2,128,640]{4,3,2,1,0:T(8,128)(2,1)} %maximum_bitcast_fusion), calls=%async_computation | async-start | bytes 2621440 | tf_op jit(solution)/shard_map/all_to_all | solution.py:265
  131.6 24.9 %copy-start.77 = (f32[2,256]{1,0:T(2,128)}, f32[2,256]{1,0:T(2,128)S(1)}, u32[]{:S(2)}) copy-start(f32[2,256]{1,0:T(2,128)S(1)} %mul.722) | copy-start | bytes 6148
  131.6 24.9 %copy-start.79 = (f32[2,256]{1,0:T(2,128)}, f32[2,256]{1,0:T(2,128)S(1)}, u32[]{:S(2)}) copy-start(f32[2,256]{1,0:T(2,128)S(1)} %mul.728) | copy-start | bytes 6148
  131.6 24.9 %copy-start.81 = (f32[2,256]{1,0:T(2,128)}, f32[2,256]{1,0:T(2,128)S(1)}, u32[]{:S(2)}) copy-start(f32[2,256]{1,0:T(2,128)S(1)} %mul.725) | copy-start | bytes 6148
  131.7 24.9 %copy-start.83 = (f32[2,256]{1,0:T(2,128)}, f32[2,256]{1,0:T(2,128)S(1)}, u32[]{:S(2)}) copy-start(f32[2,256]{1,0:T(2,128)S(1)} %mul.731) | copy-start | bytes 6148
  131.8 23.2 %copy-start.117 = (f32[2]{0:T(128)}, f32[2]{0:T(128)S(1)}, u32[]{:S(2)}) copy-start(f32[2]{0:T(128)S(1)} %dynamic_slice.231) | copy-start | bytes 28
  131.8 23.2 %copy-start.119 = (f32[2]{0:T(128)}, f32[2]{0:T(128)S(1)}, u32[]{:S(2)}) copy-start(f32[2]{0:T(128)S(1)} %dynamic-slice_negate_fusion) | copy-start | bytes 28
  192.8 21.0 %all-to-all-start.1 = ((bf16[4,1,2,128,256]{4,3,2,1,0:T(8,128)(2,1)}), bf16[4,1,2,128,256]{4,3,2,1,0:T(8,128)(2,1)}, u32[]{:S(2)}, u32[]{:S(2)}) async-start(bf16[4,1,2,128,256]{4,3,2,1,0:T(8,128)(2,1)} %bitcast.486), calls=%async_computation.1 | async-start | bytes 1048576 | tf_op jit(solution)/shard_map/all_to_all | solution.py:274
  335.4 19.3 %all-to-all-start.2 = ((bf16[4,1,2,128,256]{4,3,2,1,0:T(8,128)(2,1)}), bf16[4,1,2,128,256]{4,3,2,1,0:T(8,128)(2,1)}, u32[]{:S(2)}, u32[]{:S(2)}) async-start(bf16[4,1,2,128,256]{4,3,2,1,0:T(8,128)(2,1)} %bitcast.493), calls=%async_computation.2 | async-start | bytes 1048576 | tf_op jit(solution)/shard_map/all_to_all | solution.py:265
  346.9 113.7 %collective-permute-start.20 = (bf16[512,2048]{1,0:T(8,128)(2,1)}, bf16[512,2048]{1,0:T(8,128)(2,1)}, u32[]{:S(2)}, u32[]{:S(2)}) collective-permute-start(bf16[512,2048]{1,0:T(8,128)(2,1)} %convolution_convert_fusion.3), channel_id=1, source_target_pairs={{0,1},{1,0},{2,3},{3,2},{4,5},{5,4},{6,7},{7,6},{8,9},{9,8},{10,11... | collective-permute-start | bytes 6291464 | tf_op jit(solution)/shard_map/ppermute | solution.py:326
  347.1 110.5 %collective-permute-start.25 = (bf16[1024,1024]{1,0:T(8,128)(2,1)}, bf16[1024,1024]{1,0:T(8,128)(2,1)}, u32[]{:S(2)}, u32[]{:S(2)}) collective-permute-start(bf16[1024,1024]{1,0:T(8,128)(2,1)} %convolution_convert_fusion.7), channel_id=1, source_target_pairs={{0,1},{1,0},{2,3},{3,2},{4,5},{5,4},{6,7},{7,6},{8,9},{9,8},{10,11... | collective-permute-start | bytes 6291464 | tf_op jit(solution)/shard_map/ppermute | solution.py:326
  349.9 123.2 %collective-permute-start.30 = (bf16[512,2816]{1,0:T(8,128)(2,1)}, bf16[512,2816]{1,0:T(8,128)(2,1)}, u32[]{:S(2)}, u32[]{:S(2)}) collective-permute-start(bf16[512,2816]{1,0:T(8,128)(2,1)} %convolution_convert_fusion.1), channel_id=1, source_target_pairs={{0,1},{1,0},{2,3},{3,2},{4,5},{5,4},{6,7},{7,6},{8,9},{9,8},{10,11... | collective-permute-start | bytes 8650760 | tf_op jit(solution)/shard_map/ppermute | solution.py:326
  350.1 127.4 %collective-permute-start.40 = (bf16[1408,1024]{1,0:T(8,128)(2,1)}, bf16[1408,1024]{1,0:T(8,128)(2,1)}, u32[]{:S(2)}, u32[]{:S(2)}) collective-permute-start(bf16[1408,1024]{1,0:T(8,128)(2,1)} %convolution_convert_fusion.2), channel_id=1, source_target_pairs={{0,1},{1,0},{2,3},{3,2},{4,5},{5,4},{6,7},{7,6},{8,9},{9,8},{10,11... | collective-permute-start | bytes 8650760 | tf_op jit(solution)/shard_map/ppermute | solution.py:326
  356.2 27.5 %copy-start.23 = (f32[1,2,512,256]{3,2,1,0:T(8,128)S(1)}, f32[1,2,512,256]{3,2,1,0:T(8,128)}, u32[]{:S(2)}) copy-start(f32[1,2,512,256]{3,2,1,0:T(8,128)} %copy-done.22) | copy-start | bytes 3145732
  356.2 27.5 %copy-start.49 = (f32[1,2,512,256]{3,2,1,0:T(8,128)S(1)}, f32[1,2,512,256]{3,2,1,0:T(8,128)}, u32[]{:S(2)}) copy-start(f32[1,2,512,256]{3,2,1,0:T(8,128)} %get-tuple-element.195) | copy-start | bytes 3145732
  401.3 20.8 %all-to-all-start.3 = ((bf16[4,1,2,128,640]{4,3,2,1,0:T(8,128)(2,1)}), bf16[4,1,2,128,640]{4,3,2,1,0:T(8,128)(2,1)S(1)}, u32[]{:S(2)}, u32[]{:S(2)}) async-start(bf16[4,1,2,128,640]{4,3,2,1,0:T(8,128)(2,1)} %bitcast.408), calls=%async_computation.3 | async-start | bytes 2621440 | tf_op jit(solution)/shard_map/all_to_all | solution.py:274
  432.9 1.3 collective-permute-start
  434.2 4.5 collective-permute-start.1
  438.7 6.2 collective-permute-start.2
  445.0 4.5 collective-permute-start.3
  449.5 4.5 collective-permute-start.4
  453.9 11.7 %collective-permute-start.10 = (bf16[512,1280]{1,0:T(8,128)(2,1)}, bf16[512,1280]{1,0:T(8,128)(2,1)}, u32[]{:S(2)}, u32[]{:S(2)}) collective-permute-start(bf16[512,1280]{1,0:T(8,128)(2,1)} %convolution_convert_fusion.5), channel_id=1, source_target_pairs={{0,1},{1,0},{2,3},{3,2},{4,5},{5,4},{6,7},{7,6},{8,9},{9,8},{10,11... | collective-permute-start | bytes 3932168 | tf_op jit(solution)/shard_map/ppermute | solution.py:326
  457.6 12.5 %collective-permute-start.5 = (bf16[512,1280]{1,0:T(8,128)(2,1)}, bf16[512,1280]{1,0:T(8,128)(2,1)S(1)}, u32[]{:S(2)}, u32[]{:S(2)}) collective-permute-start(bf16[512,1280]{1,0:T(8,128)(2,1)} %convolution_convert_fusion.6), channel_id=1, source_target_pairs={{0,1},{1,0},{2,3},{3,2},{4,5},{5,4},{6,7},{7,6},{8,9},{9,8},{10,11... | collective-permute-start | bytes 3932168 | tf_op jit(solution)/shard_map/ppermute | solution.py:326
  460.6 21.2 %collective-permute-start.35 = (bf16[512,2816]{1,0:T(8,128)(2,1)S(1)}, bf16[512,2816]{1,0:T(8,128)(2,1)S(1)}, u32[]{:S(2)}, u32[]{:S(2)}) collective-permute-start(bf16[512,2816]{1,0:T(8,128)(2,1)S(1)} %copy-done.54), channel_id=1, source_target_pairs={{0,1},{1,0},{2,3},{3,2},{4,5},{5,4},{6,7},{7,6},{8,9},{9,8},{10,11... | collective-permute-start | bytes 8650760 | tf_op jit(solution)/shard_map/ppermute | solution.py:326
  467.1 19.0 %collective-permute-start.15 = (bf16[512,1552]{0,1:T(8,128)(2,1)S(1)}, bf16[512,1552]{0,1:T(8,128)(2,1)S(1)}, u32[]{:S(2)}, u32[]{:S(2)}) collective-permute-start(bf16[512,1552]{0,1:T(8,128)(2,1)S(1)} %copy-done.59), channel_id=1, source_target_pairs={{0,1},{1,0},{2,3},{3,2},{4,5},{5,4},{6,7},{7,6},{8,9},{9,8},{10,11... | collective-permute-start | bytes 4767752 | tf_op jit(solution)/shard_map/ppermute | solution.py:326
  470.0 31.9 %collective-permute-start.21 = (bf16[1,256,2048]{2,1,0:T(8,128)(2,1)}, bf16[1,256,2048]{2,1,0:T(8,128)(2,1)}, u32[]{:S(2)}, u32[]{:S(2)}) collective-permute-start(bf16[1,256,2048]{2,1,0:T(8,128)(2,1)} %dynamic-slice_bitcast_fusion.4), channel_id=1, source_target_pairs={{0,16},{8,24},{16,0},{24,8},{1,17},{9,25},{17,1},{25,9},{2,18},{10... | collective-permute-start | bytes 3145736 | tf_op jit(solution)/shard_map/ppermute | solution.py:326
  473.0 26.3 %collective-permute-start.26 = (bf16[2,256,1024]{2,1,0:T(8,128)(2,1)}, bf16[2,256,1024]{2,1,0:T(8,128)(2,1)}, u32[]{:S(2)}, u32[]{:S(2)}) collective-permute-start(bf16[2,256,1024]{2,1,0:T(8,128)(2,1)} %dynamic-slice_bitcast_fusion.3), channel_id=1, source_target_pairs={{0,8},{8,0},{16,24},{24,16},{1,9},{9,1},{17,25},{25,17},{2,10},{10... | collective-permute-start | bytes 3145736 | tf_op jit(solution)/shard_map/ppermute | solution.py:326
  477.5 37.5 %collective-permute-start.11 = (bf16[1,256,1280]{2,1,0:T(8,128)(2,1)}, bf16[1,256,1280]{2,1,0:T(8,128)(2,1)}, u32[]{:S(2)}, u32[]{:S(2)}) collective-permute-start(bf16[1,256,1280]{2,1,0:T(8,128)(2,1)} %dynamic-slice_bitcast_fusion.8), channel_id=1, source_target_pairs={{0,16},{8,24},{16,0},{24,8},{1,17},{9,25},{17,1},{25,9},{2,18},{10... | collective-permute-start | bytes 1966088 | tf_op jit(solution)/shard_map/ppermute | solution.py:326
  481.8 31.6 %collective-permute-start.6 = (bf16[2,128,1280]{2,1,0:T(8,128)(2,1)}, bf16[2,128,1280]{2,1,0:T(8,128)(2,1)}, u32[]{:S(2)}, u32[]{:S(2)}) collective-permute-start(bf16[2,128,1280]{2,1,0:T(8,128)(2,1)} %dynamic-slice_bitcast_fusion.9), channel_id=1, source_target_pairs={{0,8},{8,0},{16,24},{24,16},{1,9},{9,1},{17,25},{25,17},{2,10},{10... | collective-permute-start | bytes 1966088 | tf_op jit(solution)/shard_map/ppermute | solution.py:326
  486.1 144.3 %collective-permute-start.36 = (bf16[8,32,2816]{2,1,0:T(8,128)(2,1)}, bf16[8,32,2816]{2,1,0:T(8,128)(2,1)}, u32[]{:S(2)}, u32[]{:S(2)}) collective-permute-start(bf16[8,32,2816]{2,1,0:T(8,128)(2,1)} %dynamic-slice_bitcast_fusion.1), channel_id=1, source_target_pairs={{0,2},{1,3},{2,0},{3,1},{4,6},{5,7},{6,4},{7,5},{8,10},{9,11},{10,... | collective-permute-start | bytes 4325384 | tf_op jit(solution)/shard_map/ppermute | solution.py:326
  499.3 135.5 %collective-permute-start.31 = (bf16[1,256,2816]{2,1,0:T(8,128)(2,1)}, bf16[1,256,2816]{2,1,0:T(8,128)(2,1)S(1)}, u32[]{:S(2)}, u32[]{:S(2)}) collective-permute-start(bf16[1,256,2816]{2,1,0:T(8,128)(2,1)} %dynamic-slice_bitcast_fusion.2), channel_id=1, source_target_pairs={{0,16},{8,24},{16,0},{24,8},{1,17},{9,25},{17,1},{25,9},{2,18},{10... | collective-permute-start | bytes 4325384 | tf_op jit(solution)/shard_map/ppermute | solution.py:326
  501.9 134.3 %collective-permute-start.41 = (bf16[2,352,1024]{2,1,0:T(8,128)(2,1)S(1)}, bf16[2,352,1024]{2,1,0:T(8,128)(2,1)S(1)}, u32[]{:S(2)}, u32[]{:S(2)}) collective-permute-start(bf16[2,352,1024]{2,1,0:T(8,128)(2,1)S(1)} %copy-done.60), channel_id=1, source_target_pairs={{0,8},{8,0},{16,24},{24,16},{1,9},{9,1},{17,25},{25,17},{2,10},{10... | collective-permute-start | bytes 4325384 | tf_op jit(solution)/shard_map/ppermute | solution.py:326
  513.4 57.0 %collective-permute-start.22 = (bf16[4,32,2048]{2,1,0:T(8,128)(2,1)S(1)}, bf16[4,32,2048]{2,1,0:T(8,128)(2,1)S(1)}, u32[]{:S(2)}, u32[]{:S(2)}) collective-permute-start(bf16[4,32,2048]{2,1,0:T(8,128)(2,1)S(1)} %dynamic-slice_bitcast_fusion.10), channel_id=1, source_target_pairs={{0,2},{1,3},{2,0},{3,1},{4,6},{5,7},{6,4},{7,5},{8,10},{9,11},{10,... | collective-permute-start | bytes 1572872 | tf_op jit(solution)/shard_map/ppermute | solution.py:326
  515.1 32.7 %collective-permute-start.7 = (bf16[1,128,1280]{2,1,0:T(8,128)(2,1)S(1)}, bf16[1,128,1280]{2,1,0:T(8,128)(2,1)S(1)}, u32[]{:S(2)}, u32[]{:S(2)}) collective-permute-start(bf16[1,128,1280]{2,1,0:T(8,128)(2,1)S(1)} %constant_dynamic-slice_fusion.17), channel_id=1, source_target_pairs={{0,16},{8,24},{16,0},{24,8},{1,17},{9,25},{17,1},{25,9},{2,18},{10... | collective-permute-start | bytes 983048 | tf_op jit(solution)/shard_map/ppermute | solution.py:326
  547.8 9.3 %collective-permute-start.12 = (bf16[4,32,1280]{2,1,0:T(8,128)(2,1)S(1)}, bf16[4,32,1280]{2,1,0:T(8,128)(2,1)S(1)}, u32[]{:S(2)}, u32[]{:S(2)}) collective-permute-start(bf16[4,32,1280]{2,1,0:T(8,128)(2,1)S(1)} %dynamic-slice_bitcast_fusion.14), channel_id=1, source_target_pairs={{0,2},{1,3},{2,0},{3,1},{4,6},{5,7},{6,4},{7,5},{8,10},{9,11},{10,... | collective-permute-start | bytes 983048 | tf_op jit(solution)/shard_map/ppermute | solution.py:326
  557.1 12.6 %collective-permute-start.27 = (bf16[1,256,1024]{2,1,0:T(8,128)(2,1)S(1)}, bf16[1,256,1024]{2,1,0:T(8,128)(2,1)S(1)}, u32[]{:S(2)}, u32[]{:S(2)}) collective-permute-start(bf16[1,256,1024]{2,1,0:T(8,128)(2,1)S(1)} %constant_dynamic-slice_fusion.10), channel_id=1, source_target_pairs={{0,16},{8,24},{16,0},{24,8},{1,17},{9,25},{17,1},{25,9},{2,18},{10... | collective-permute-start | bytes 1572872 | tf_op jit(solution)/shard_map/ppermute | solution.py:326
  558.7 33.3 %copy-start.35 = (bf16[512,1552]{1,0:T(8,128)(2,1)S(1)}, bf16[512,1552]{1,0:T(8,128)(2,1)}, u32[]{:S(2)}) copy-start(bf16[512,1552]{1,0:T(8,128)(2,1)} %copy.229) | copy-start | bytes 4767748
  569.7 22.3 %collective-permute-start.16 = (bf16[8,32,1552]{2,1,0:T(8,128)(2,1)S(1)}, bf16[8,32,1552]{2,1,0:T(8,128)(2,1)S(1)}, u32[]{:S(2)}, u32[]{:S(2)}) collective-permute-start(bf16[8,32,1552]{2,1,0:T(8,128)(2,1)S(1)} %dynamic-slice_bitcast_fusion.5), channel_id=1, source_target_pairs={{0,2},{1,3},{2,0},{3,1},{4,6},{5,7},{6,4},{7,5},{8,10},{9,11},{10,... | collective-permute-start | bytes 2383880 | tf_op jit(solution)/shard_map/ppermute | solution.py:326
  570.4 21.9 %collective-permute-start.13 = (bf16[2,32,1280]{2,1,0:T(8,128)(2,1)S(1)}, bf16[2,32,1280]{2,1,0:T(8,128)(2,1)S(1)}, u32[]{:S(2)}, u32[]{:S(2)}) collective-permute-start(bf16[2,32,1280]{2,1,0:T(8,128)(2,1)S(1)} %dynamic-slice_bitcast_fusion.18), channel_id=1, source_target_pairs={{0,4},{1,5},{2,6},{3,7},{4,0},{5,1},{6,2},{7,3},{8,12},{9,13},{10,... | collective-permute-start | bytes 491528 | tf_op jit(solution)/shard_map/ppermute | solution.py:326
  592.0 6.6 collective-permute-start.8
  592.3 24.9 %collective-permute-start.23 = (bf16[2,32,2048]{2,1,0:T(8,128)(2,1)S(1)}, bf16[2,32,2048]{2,1,0:T(8,128)(2,1)S(1)}, u32[]{:S(2)}, u32[]{:S(2)}) collective-permute-start(bf16[2,32,2048]{2,1,0:T(8,128)(2,1)S(1)} %dynamic-slice_bitcast_fusion.16), channel_id=1, source_target_pairs={{0,4},{1,5},{2,6},{3,7},{4,0},{5,1},{6,2},{7,3},{8,12},{9,13},{10,... | collective-permute-start | bytes 786440 | tf_op jit(solution)/shard_map/ppermute | solution.py:326
  598.6 4.4 collective-permute-start.14
  603.0 6.2 collective-permute-start.9
  609.2 6.4 collective-permute-start.28
  615.6 14.1 %collective-permute-start.17 = (bf16[2,64,1552]{2,1,0:T(8,128)(2,1)S(1)}, bf16[2,64,1552]{2,1,0:T(8,128)(2,1)S(1)}, u32[]{:S(2)}, u32[]{:S(2)}) collective-permute-start(bf16[2,64,1552]{2,1,0:T(8,128)(2,1)S(1)} %dynamic-slice_bitcast_fusion.11), channel_id=1, source_target_pairs={{0,8},{8,0},{16,24},{24,16},{1,9},{9,1},{17,25},{25,17},{2,10},{10... | collective-permute-start | bytes 1191944 | tf_op jit(solution)/shard_map/ppermute | solution.py:326
  617.2 6.8 collective-permute-start.29
  624.0 5.0 collective-permute-start.24
  629.8 7.1 %collective-permute-start.18 = (bf16[1,64,1552]{2,1,0:T(8,128)(2,1)S(1)}, bf16[1,64,1552]{2,1,0:T(8,128)(2,1)S(1)}, u32[]{:S(2)}, u32[]{:S(2)}) collective-permute-start(bf16[1,64,1552]{2,1,0:T(8,128)(2,1)S(1)} %constant_dynamic-slice_fusion.14), channel_id=1, source_target_pairs={{0,16},{8,24},{16,0},{24,8},{1,17},{9,25},{17,1},{25,9},{2,18},{10... | collective-permute-start | bytes 595976 | tf_op jit(solution)/shard_map/ppermute | solution.py:326
  633.2 18.5 %collective-permute-start.37 = (bf16[2,64,2816]{2,1,0:T(8,128)(2,1)}, bf16[2,64,2816]{2,1,0:T(8,128)(2,1)}, u32[]{:S(2)}, u32[]{:S(2)}) collective-permute-start(bf16[2,64,2816]{2,1,0:T(8,128)(2,1)} %dynamic-slice_bitcast_fusion.6), channel_id=1, source_target_pairs={{0,8},{8,0},{16,24},{24,16},{1,9},{9,1},{17,25},{25,17},{2,10},{10... | collective-permute-start | bytes 2162696 | tf_op jit(solution)/shard_map/ppermute | solution.py:326
  636.2 17.6 %collective-permute-start.32 = (bf16[4,32,2816]{2,1,0:T(8,128)(2,1)}, bf16[4,32,2816]{2,1,0:T(8,128)(2,1)}, u32[]{:S(2)}, u32[]{:S(2)}) collective-permute-start(bf16[4,32,2816]{2,1,0:T(8,128)(2,1)} %dynamic-slice_bitcast_fusion.7), channel_id=1, source_target_pairs={{0,2},{1,3},{2,0},{3,1},{4,6},{5,7},{6,4},{7,5},{8,10},{9,11},{10,... | collective-permute-start | bytes 2162696 | tf_op jit(solution)/shard_map/ppermute | solution.py:326
  637.0 12.6 %collective-permute-start.19 = (bf16[1,32,1552]{2,1,0:T(8,128)(2,1)S(1)}, bf16[1,32,1552]{2,1,0:T(8,128)(2,1)S(1)}, u32[]{:S(2)}, u32[]{:S(2)}) collective-permute-start(bf16[1,32,1552]{2,1,0:T(8,128)(2,1)S(1)} %dynamic-slice_bitcast_fusion.20), channel_id=1, source_target_pairs={{0,4},{1,5},{2,6},{3,7},{4,0},{5,1},{6,2},{7,3},{8,12},{9,13},{10,... | collective-permute-start | bytes 297992 | tf_op jit(solution)/shard_map/ppermute | solution.py:326
  639.9 18.7 %collective-permute-start.42 = (bf16[1,352,1024]{2,1,0:T(8,128)(2,1)}, bf16[1,352,1024]{2,1,0:T(8,128)(2,1)}, u32[]{:S(2)}, u32[]{:S(2)}) collective-permute-start(bf16[1,352,1024]{2,1,0:T(8,128)(2,1)} %constant_dynamic-slice_fusion.2), channel_id=1, source_target_pairs={{0,16},{8,24},{16,0},{24,8},{1,17},{9,25},{17,1},{25,9},{2,18},{10... | collective-permute-start | bytes 2162696 | tf_op jit(solution)/shard_map/ppermute | solution.py:326
  653.3 7.5 %collective-permute-start.38 = (bf16[1,64,2816]{2,1,0:T(8,128)(2,1)S(1)}, bf16[1,64,2816]{2,1,0:T(8,128)(2,1)S(1)}, u32[]{:S(2)}, u32[]{:S(2)}) collective-permute-start(bf16[1,64,2816]{2,1,0:T(8,128)(2,1)S(1)} %constant_dynamic-slice_fusion.5), channel_id=1, source_target_pairs={{0,16},{8,24},{16,0},{24,8},{1,17},{9,25},{17,1},{25,9},{2,18},{10... | collective-permute-start | bytes 1081352 | tf_op jit(solution)/shard_map/ppermute | solution.py:326
  655.1 22.5 %collective-permute-start.33 = (bf16[2,32,2816]{2,1,0:T(8,128)(2,1)S(1)}, bf16[2,32,2816]{2,1,0:T(8,128)(2,1)S(1)}, u32[]{:S(2)}, u32[]{:S(2)}) collective-permute-start(bf16[2,32,2816]{2,1,0:T(8,128)(2,1)S(1)} %dynamic-slice_bitcast_fusion.13), channel_id=1, source_target_pairs={{0,4},{1,5},{2,6},{3,7},{4,0},{5,1},{6,2},{7,3},{8,12},{9,13},{10,... | collective-permute-start | bytes 1081352 | tf_op jit(solution)/shard_map/ppermute | solution.py:326
  660.0 19.3 %collective-permute-start.43 = (bf16[2,88,1024]{2,1,0:T(8,128)(2,1)S(1)}, bf16[2,88,1024]{2,1,0:T(8,128)(2,1)S(1)}, u32[]{:S(2)}, u32[]{:S(2)}) collective-permute-start(bf16[2,88,1024]{2,1,0:T(8,128)(2,1)S(1)} %dynamic-slice_bitcast_fusion.12), channel_id=1, source_target_pairs={{0,2},{1,3},{2,0},{3,1},{4,6},{5,7},{6,4},{7,5},{8,10},{9,11},{10,... | collective-permute-start | bytes 1081352 | tf_op jit(solution)/shard_map/ppermute | solution.py:326
  660.9 19.5 %collective-permute-start.39 = (bf16[1,32,2816]{2,1,0:T(8,128)(2,1)S(1)}, bf16[1,32,2816]{2,1,0:T(8,128)(2,1)S(1)}, u32[]{:S(2)}, u32[]{:S(2)}) collective-permute-start(bf16[1,32,2816]{2,1,0:T(8,128)(2,1)S(1)} %dynamic-slice_bitcast_fusion.17), channel_id=1, source_target_pairs={{0,4},{1,5},{2,6},{3,7},{4,0},{5,1},{6,2},{7,3},{8,12},{9,13},{10,... | collective-permute-start | bytes 540680 | tf_op jit(solution)/shard_map/ppermute | solution.py:326
  677.7 5.6 collective-permute-start.34
  679.4 7.2 %collective-permute-start.44 = (bf16[1,88,1024]{2,1,0:T(8,128)(2,1)S(1)}, bf16[1,88,1024]{2,1,0:T(8,128)(2,1)S(1)}, u32[]{:S(2)}, u32[]{:S(2)}) collective-permute-start(bf16[1,88,1024]{2,1,0:T(8,128)(2,1)S(1)} %constant_dynamic-slice_fusion.1), channel_id=1, source_target_pairs={{0,4},{1,5},{2,6},{3,7},{4,0},{5,1},{6,2},{7,3},{8,12},{9,13},{10,... | collective-permute-start | bytes 540680 | tf_op jit(solution)/shard_map/ppermute | solution.py:326
  (116 other events, 632.9 us)
Sparse Core Ops, SparseCore 0:
  11.5 100.0 all-gather.3
  115.0 88.0 all-gather.5
  206.5 89.4 all-gather.7
